TPU v7x, 256 devices: a whole 4x4x8 slice. The times are simulated.
256 devices in a mesh: blk: 32 (over y_hi, z, core), grp: 8 (over y_lo, x).
Axes of the slice: x: 4, y: 4 (y_hi: 2, y_lo: 2; y = y_hi * 2 + y_lo), z: 8, core: 2. Of those that a mesh axis runs over, the one named last changes fastest.
Arguments:
- teacher_image: bfloat16 [1280, 8192], P('grp', 'blk'), may hold values from -10.968894 to 10.968894
- teacher_text: bfloat16 [8192, 1280], P(('blk', 'grp')), may hold values from -10.968894 to 10.968894
- student_image: bfloat16 [512, 8192], P('grp', 'blk'), may hold values from -13.792653 to 13.792653
- student_text: bfloat16 [8192, 512], P(('blk', 'grp')), may hold values from -13.792653 to 13.792653
Outputs:
- image_grad: float32 [8192, 512], P(('blk', 'grp'))
- text_grad: float32 [8192, 512], P(('blk', 'grp'))
- row_loss: float32 [8192], P(('blk', 'grp'))
- column_loss: float32 [8192], P(('blk', 'grp'))
All inputs are finite; a program needn't handle non-finite values.
Results may differ from a plain program's by a relative error of at most 0.004.
Values may be sent and summed in bfloat16 or wider, within the bound.
A program may use at most 64 MiB of HBM per device.

v0:
```python
import jax
import jax.numpy as jnp
from jax import lax
from jax.sharding import PartitionSpec as P

floor_value = -1e30


def for_sending(array):
    return jax.tree.map(lambda a: a.astype(jnp.bfloat16) if a.dtype == jnp.float32 else a, array)


def shifted(array, axis, by):
    length = lax.axis_size(axis)
    return lax.ppermute(array, axis, [(i, (i + by) % length) for i in range(length)])


def combined_all(array, axis, combine):
    everything = jax.tree.map(lambda part: lax.all_gather(part, axis), array)
    leading = jax.tree.map(lambda part: part[0], everything)

    def turn(k, so_far):
        return combine(so_far, jax.tree.map(lambda part: part[k], everything))

    return lax.fori_loop(1, lax.axis_size(axis), turn, leading)


def similarity(left, right, scale):
    return (
        lax.dot_general(left, right, (((1,), (0,)), ((), ())), preferred_element_type=jnp.float32)
        * scale
    )


def contract_rows(left, right):
    return lax.dot_general(
        left, right, (((0,), (0,)), ((), ())), preferred_element_type=jnp.float32
    )


def contract_columns(left, right):
    return lax.dot_general(
        left, right, (((1,), (1,)), ((), ())), preferred_element_type=jnp.float32
    )


def tile_stats(logits, axis):
    highest = jnp.max(logits, axis=axis)
    return (highest, jnp.sum(jnp.exp(logits - jnp.expand_dims(highest, axis)), axis=axis))


def blend_stats(earlier, later):
    merged = []
    for offset in (0, 2):
        highest = jnp.maximum(earlier[offset], later[offset])
        merged.append(highest)
        merged.append(
            earlier[offset + 1] * jnp.exp(earlier[offset] - highest)
            + later[offset + 1] * jnp.exp(later[offset] - highest)
        )
    return tuple(merged)


def move_texts(parcels):
    return (shifted(for_sending(parcels[0]), "blk", 1),)


def move_sums(parcels):
    return (shifted(parcels[0], "blk", 1),)


def block_anchor(position, heading, step_index, cycle_size):
    return jnp.mod(position - heading * step_index, cycle_size)


def body(teacher_image, teacher_text, student_image, student_text):
    row_count = teacher_text.shape[0]
    student_width = student_text.shape[1]
    cycle_size = lax.axis_size("blk")
    position = lax.axis_index("blk")
    member = lax.axis_index("grp")
    scale_t = teacher_text.shape[1] ** (-0.5)
    scale_s = student_width ** (-0.5)
    pair_count = row_count * cycle_size * lax.axis_size("grp")
    images_t, images_s = (
        lax.all_gather(teacher_image, "grp", axis=0, tiled=True),
        lax.all_gather(student_image, "grp", axis=0, tiled=True),
    )
    span = images_t.shape[1]
    lanes = ((0, row_count, 1),)
    first_parcels = tuple(((teacher_text, student_text) for begin, width, heading in lanes))

    def texts_of(parcels, lane_number):
        return parcels[lane_number]

    column_buffer = jnp.zeros((cycle_size, 4, row_count), jnp.float32)
    lowest = jnp.full((span,), floor_value, jnp.float32)
    nothing = jnp.zeros((span,), jnp.float32)
    stored = jnp.zeros((1, 1, 1), jnp.float32)

    def first_step(step_index, carry):
        parcels, row_stats, column_buffer, stored = carry
        for lane_number, (begin, width, heading) in enumerate(lanes):
            anchor = block_anchor(position, heading, step_index, cycle_size)
            texts = texts_of(parcels, lane_number)
            logit_t = similarity(texts[0], images_t, scale_t)
            logit_s = similarity(texts[1], images_s, scale_s)
            row_stats = blend_stats(row_stats, tile_stats(logit_t, 0) + tile_stats(logit_s, 0))
            column = jnp.stack(tile_stats(logit_t, 1) + tile_stats(logit_s, 1))
            column_buffer = lax.dynamic_update_slice(
                column_buffer, column[None], (anchor, jnp.int32(0), jnp.int32(begin))
            )
        return (move_texts(parcels), row_stats, column_buffer, stored)

    start = (first_parcels, (lowest, nothing, lowest, nothing), column_buffer, stored)
    parcels, row_stats, column_buffer, stored = lax.fori_loop(0, cycle_size, first_step, start)
    row_stats = combined_all(row_stats, "grp", blend_stats)
    row_lse_t = row_stats[0] + jnp.log(row_stats[1])
    row_lse_s = row_stats[2] + jnp.log(row_stats[3])
    arrived = lax.all_to_all(column_buffer, "blk", split_axis=0, concat_axis=0, tiled=True)
    top_t = jnp.max(arrived[:, 0], axis=0)
    total_t = jnp.sum(arrived[:, 1] * jnp.exp(arrived[:, 0] - top_t[None, :]), axis=0)
    top_s = jnp.max(arrived[:, 2], axis=0)
    total_s = jnp.sum(arrived[:, 3] * jnp.exp(arrived[:, 2] - top_s[None, :]), axis=0)
    own_lse = jnp.stack([top_t + jnp.log(total_t), top_s + jnp.log(total_s)])
    every_lse = lax.all_gather(own_lse, "blk", axis=1, tiled=True)
    second_parcels = tuple(((teacher_text, student_text) for begin, width, heading in lanes))
    zero_sums = tuple(
        (
            (jnp.zeros((width, student_width), jnp.float32), jnp.zeros((width,), jnp.float32))
            for begin, width, heading in lanes
        )
    )

    def second_step(step_index, carry):
        parcels, lane_sums, image_acc, row_acc = carry
        updated = []
        for lane_number, (begin, width, heading) in enumerate(lanes):
            anchor = block_anchor(position, heading, step_index, cycle_size)
            texts = texts_of(parcels, lane_number)
            block_s = texts[-1]
            logit_t = similarity(texts[0], images_t, scale_t)
            logit_s = similarity(block_s, images_s, scale_s)
            lse_cols = lax.dynamic_slice(
                every_lse, (jnp.int32(0), anchor * row_count + begin), (2, width)
            )
            prob_t = jnp.exp(logit_t - row_lse_t[None, :])
            prob_s = jnp.exp(logit_s - row_lse_s[None, :])
            share_t = jnp.exp(logit_t - lse_cols[0][:, None])
            share_s = jnp.exp(logit_s - lse_cols[1][:, None])
            gap = logit_t - logit_s
            weights = (pair_count * (prob_s - prob_t + share_s - share_t)).astype(jnp.bfloat16)
            image_acc = image_acc + contract_rows(weights, block_s)
            row_acc = row_acc + jnp.sum(prob_t * gap, axis=0)
            text_piece = contract_columns(weights, images_s)
            column_piece = jnp.sum(share_t * gap, axis=1)
            grad_sum, divergence = lane_sums[lane_number]
            updated.append((grad_sum + text_piece, divergence + column_piece))
        new_sums = move_sums(tuple(updated))
        return (move_texts(parcels), new_sums, image_acc, row_acc)

    start = (
        second_parcels,
        zero_sums,
        jnp.zeros((span, student_width), jnp.float32),
        jnp.zeros((span,), jnp.float32),
    )
    parcels, lane_sums, image_acc, row_acc = lax.fori_loop(0, cycle_size, second_step, start)
    image_part, row_part = (
        lax.psum_scatter(image_acc, "grp", scatter_dimension=0, tiled=True),
        lax.psum_scatter(row_acc, "grp", scatter_dimension=0, tiled=True),
    )
    own_row_t = lax.dynamic_slice_in_dim(row_lse_t, member * row_count, row_count)
    own_row_s = lax.dynamic_slice_in_dim(row_lse_s, member * row_count, row_count)
    row_loss = row_part - own_row_t + own_row_s
    image_grad = image_part * scale_s
    text_total = jnp.concatenate([pair_sums[0] for pair_sums in lane_sums], axis=0)
    column_kl = jnp.concatenate([pair_sums[1] for pair_sums in lane_sums], axis=0)
    text_grad = text_total * scale_s
    column_loss = column_kl - own_lse[0] + own_lse[1]
    return (image_grad, text_grad, row_loss, column_loss)


def solution(mesh):
    in_specs = (P("grp", "blk"), P(("blk", "grp"), None), P("grp", "blk"), P(("blk", "grp"), None))
    out_specs = (
        P(("blk", "grp"), None),
        P(("blk", "grp"), None),
        P(("blk", "grp")),
        P(("blk", "grp")),
    )
    return jax.shard_map(body, mesh=mesh, in_specs=in_specs, out_specs=out_specs, check_vma=False)
```

profile of v0, /device:TPU:1, one launch (start us, length us, event | category | flops | bytes accessed | tf_op | source)
XLA Modules:
  0.0 758.0 jit_solution(9986654351797190870)
XLA Ops:
  8.2 25.0 %all_gather.34 = bf16[1280,256]{1,0:T(8,128)(2,1)S(1)} all-gather(bf16[160,256]{1,0:T(8,128)(2,1)S(1)} %copy-done.7), channel_id=1, replica_groups=mesh['blk'=32,'grp'=8] {'grp'}, dimensions={0}, use_global_device_ids=true | all-gather | bytes 737280 | tf_op jit(solution)/shard_map/all_gather | solution.py:86
  33.2 22.1 %all_gather.33 = bf16[512,256]{1,0:T(8,128)(2,1)S(1)} all-gather(bf16[64,256]{1,0:T(8,128)(2,1)S(1)} %copy-done.12), channel_id=1, replica_groups=mesh['blk'=32,'grp'=8] {'grp'}, dimensions={0}, use_global_device_ids=true | all-gather | bytes 294912 | tf_op jit(solution)/shard_map/all_gather | solution.py:87
  56.3 260.7 %while.76 = (s32[]{:T(128)}, bf16[32,1280]{1,0:T(8,128)(2,1)S(1)}, bf16[32,512]{1,0:T(8,128)(2,1)S(1)}, f32[256]{0:T(256)S(1)}, f32[256]{0:T(256)S(1)}, /*index=...) while((s32[]{:T(128)}, bf16[32,1280]{1,0:T(8,128)(2,1)S(1)}, ...), condition=%wide.region_9.10_spmd.clone, body=%wide.region_0.9_spmd.clone.sunk | while | flops 29478148 | bytes 1875078 | solution.py:116
  56.3 14.1 %collective-permute-start = (bf16[32,1280]{1,0:T(8,128)(2,1)S(1)}, bf16[32,1280]{1,0:T(8,128)(2,1)S(1)}, u32[]{:S(2)}, u32[]{:S(2)}) collective-permute-start(bf16[32,1280]{1,0:T(8,128)(2,1)S(1)} %copy.40), channel_id=1, source_target_pairs={{0,8},{8,16},{16,24},{24,32},{32,40},{40,48},{48,56},{56,64},{64,7... | collective-permute-start | bytes 245768 | tf_op jit(solution)/shard_map/while/body/eval_jaxpr/ppermute | solution.py:15
  317.6 10.5 %all-to-all-start = ((f32[32,1,128]{2,1,0:T(1,128)}), f32[32,1,128]{2,1,0:T(1,128)S(1)}, u32[]{:S(2)}, u32[]{:S(2)}) async-start(f32[32,1,128]{2,1,0:T(1,128)} %reshape.81), calls=%async_computation | async-start | bytes 32768 | tf_op jit(solution)/shard_map/all_to_all | solution.py:120
  328.2 13.5 %all-gather.7 = f32[8,1,256]{2,1,0:T(1,128)S(1)} all-gather(f32[1,1,256]{2,1,0:T(1,128)S(1)} %bitcast.133), channel_id=5, replica_groups=mesh['blk'=32,'grp'=8] {'grp'}, dimensions={0}, use_global_device_ids=true | all-gather | bytes 9216 | tf_op jit(solution)/shard_map/all_gather | solution.py:19
  342.3 11.6 %all-gather.4 = f32[8,1,256]{2,1,0:T(1,128)S(1)} all-gather(f32[1,1,256]{2,1,0:T(1,128)S(1)} %bitcast.130), channel_id=2, replica_groups=mesh['blk'=32,'grp'=8] {'grp'}, dimensions={0}, use_global_device_ids=true | all-gather | bytes 9216 | tf_op jit(solution)/shard_map/all_gather | solution.py:19
  354.5 13.3 %all-gather.5 = f32[8,1,256]{2,1,0:T(1,128)S(1)} all-gather(f32[1,1,256]{2,1,0:T(1,128)S(1)} %bitcast.131), channel_id=3, replica_groups=mesh['blk'=32,'grp'=8] {'grp'}, dimensions={0}, use_global_device_ids=true | all-gather | bytes 9216 | tf_op jit(solution)/shard_map/all_gather | solution.py:19
  368.4 11.6 %all-gather.6 = f32[8,1,256]{2,1,0:T(1,128)S(1)} all-gather(f32[1,1,256]{2,1,0:T(1,128)S(1)} %bitcast.132), channel_id=4, replica_groups=mesh['blk'=32,'grp'=8] {'grp'}, dimensions={0}, use_global_device_ids=true | all-gather | bytes 9216 | tf_op jit(solution)/shard_map/all_gather | solution.py:19
  383.7 56.9 %all-gather.8 = f32[32,32,2]{1,2,0:T(2,128)S(1)} all-gather(f32[1,32,2]{1,2,0:T(2,128)S(1)} %maximum_bitcast_fusion.1), channel_id=1, replica_groups=mesh['blk'=32,'grp'=8] {'blk'}, dimensions={0}, use_global_device_ids=true | all-gather | bytes 8448 | tf_op jit(solution)/shard_map/all_gather | solution.py:126
  441.4 271.9 %while.77 = (s32[]{:T(128)}, bf16[32,1280]{1,0:T(8,128)(2,1)S(1)}, bf16[32,512]{1,0:T(8,128)(2,1)S(1)}, f32[32,512]{1,0:T(8,128)S(1)}, f32[32]{0:T(128)S(1)}, /*...) while((s32[]{:T(128)}, bf16[32,1280]{1,0:T(8,128)(2,1)S(1)}, ...), condition=%wide.region_19.20_spmd.clone, body=%wide.region_16.19_spmd.clone.sunk | while | flops 46547216 | bytes 3580667 | solution.py:168
  453.5 7.2 collective-permute-done.5
  462.3 7.2 collective-permute-done.5
  471.0 7.2 collective-permute-done.5
  479.7 7.2 collective-permute-done.5
  540.6 7.2 collective-permute-done.5
  549.3 7.2 collective-permute-done.5
  592.9 7.2 collective-permute-done.5
  610.3 7.2 collective-permute-done.5
  619.0 7.2 collective-permute-done.5
  680.0 7.2 collective-permute-done.5
  688.7 7.2 collective-permute-done.5
  716.0 14.6 %all-reduce = f32[256]{0:T(256)S(1)} all-reduce(f32[256]{0:T(256)S(1)} %get-tuple-element.819), channel_id=7, replica_groups=mesh['blk'=32,'grp'=8] {'grp'}, use_global_device_ids=true, to_apply=%region_21.22.clone | all-reduce | flops 256 | bytes 2048
  732.4 17.3 %reduce-scatter.2.cloned.1.call-done = f32[32,512]{1,0:T(8,128)} async-done(((f32[256,512]{1,0:T(8,128)}), f32[32,512]{1,0:T(8,128)}) %reduce-scatter.2.cloned.1.call-update) | async-done | bytes 65552 | tf_op jit(solution)/shard_map/reduce_scatter | solution.py:170
  (1059 shorter events, 447.8 us)
Async XLA Ops:
  56.3 15.9 %collective-permute-start = (bf16[32,1280]{1,0:T(8,128)(2,1)S(1)}, bf16[32,1280]{1,0:T(8,128)(2,1)S(1)}, u32[]{:S(2)}, u32[]{:S(2)}) collective-permute-start(bf16[32,1280]{1,0:T(8,128)(2,1)S(1)} %copy.40), channel_id=1, source_target_pairs={{0,8},{8,16},{16,24},{24,32},{32,40},{40,48},{48,56},{56,64},{64,7... | collective-permute-start | bytes 245768 | tf_op jit(solution)/shard_map/while/body/eval_jaxpr/ppermute | solution.py:15
  317.6 64.5 %all-to-all-start = ((f32[32,1,128]{2,1,0:T(1,128)}), f32[32,1,128]{2,1,0:T(1,128)S(1)}, u32[]{:S(2)}, u32[]{:S(2)}) async-start(f32[32,1,128]{2,1,0:T(1,128)} %reshape.81), calls=%async_computation | async-start | bytes 32768 | tf_op jit(solution)/shard_map/all_to_all | solution.py:120
  328.1 421.5 %reduce-scatter.2.cloned.1.call-start = ((), (), s32[]{:S(2)}) async-start(), calls=%async_computation.2 | async-start | bytes 589824 | tf_op jit(solution)/shard_map/reduce_scatter | solution.py:170
  452.1 8.7 %collective-permute-start.3 = (bf16[32,512]{1,0:T(8,128)(2,1)S(1)}, bf16[32,512]{1,0:T(8,128)(2,1)S(1)}, u32[]{:S(2)}, u32[]{:S(2)}) collective-permute-start(bf16[32,512]{1,0:T(8,128)(2,1)S(1)} %copy.79), channel_id=1, source_target_pairs={{0,8},{8,16},{16,24},{24,32},{32,40},{40,48},{48,56},{56,64},{64,7... | collective-permute-start | bytes 98312 | tf_op jit(solution)/shard_map/while/body/eval_jaxpr/ppermute | solution.py:15
  460.8 8.7 %collective-permute-start.3 = (bf16[32,512]{1,0:T(8,128)(2,1)S(1)}, bf16[32,512]{1,0:T(8,128)(2,1)S(1)}, u32[]{:S(2)}, u32[]{:S(2)}) collective-permute-start(bf16[32,512]{1,0:T(8,128)(2,1)S(1)} %copy.79), channel_id=1, source_target_pairs={{0,8},{8,16},{16,24},{24,32},{32,40},{40,48},{48,56},{56,64},{64,7... | collective-permute-start | bytes 98312 | tf_op jit(solution)/shard_map/while/body/eval_jaxpr/ppermute | solution.py:15
  469.5 8.7 %collective-permute-start.3 = (bf16[32,512]{1,0:T(8,128)(2,1)S(1)}, bf16[32,512]{1,0:T(8,128)(2,1)S(1)}, u32[]{:S(2)}, u32[]{:S(2)}) collective-permute-start(bf16[32,512]{1,0:T(8,128)(2,1)S(1)} %copy.79), channel_id=1, source_target_pairs={{0,8},{8,16},{16,24},{24,32},{32,40},{40,48},{48,56},{56,64},{64,7... | collective-permute-start | bytes 98312 | tf_op jit(solution)/shard_map/while/body/eval_jaxpr/ppermute | solution.py:15
  478.2 8.7 %collective-permute-start.3 = (bf16[32,512]{1,0:T(8,128)(2,1)S(1)}, bf16[32,512]{1,0:T(8,128)(2,1)S(1)}, u32[]{:S(2)}, u32[]{:S(2)}) collective-permute-start(bf16[32,512]{1,0:T(8,128)(2,1)S(1)} %copy.79), channel_id=1, source_target_pairs={{0,8},{8,16},{16,24},{24,32},{32,40},{40,48},{48,56},{56,64},{64,7... | collective-permute-start | bytes 98312 | tf_op jit(solution)/shard_map/while/body/eval_jaxpr/ppermute | solution.py:15
  495.6 8.7 %collective-permute-start.3 = (bf16[32,512]{1,0:T(8,128)(2,1)S(1)}, bf16[32,512]{1,0:T(8,128)(2,1)S(1)}, u32[]{:S(2)}, u32[]{:S(2)}) collective-permute-start(bf16[32,512]{1,0:T(8,128)(2,1)S(1)} %copy.79), channel_id=1, source_target_pairs={{0,8},{8,16},{16,24},{24,32},{32,40},{40,48},{48,56},{56,64},{64,7... | collective-permute-start | bytes 98312 | tf_op jit(solution)/shard_map/while/body/eval_jaxpr/ppermute | solution.py:15
  504.3 8.7 %collective-permute-start.3 = (bf16[32,512]{1,0:T(8,128)(2,1)S(1)}, bf16[32,512]{1,0:T(8,128)(2,1)S(1)}, u32[]{:S(2)}, u32[]{:S(2)}) collective-permute-start(bf16[32,512]{1,0:T(8,128)(2,1)S(1)} %copy.79), channel_id=1, source_target_pairs={{0,8},{8,16},{16,24},{24,32},{32,40},{40,48},{48,56},{56,64},{64,7... | collective-permute-start | bytes 98312 | tf_op jit(solution)/shard_map/while/body/eval_jaxpr/ppermute | solution.py:15
  521.7 8.7 %collective-permute-start.3 = (bf16[32,512]{1,0:T(8,128)(2,1)S(1)}, bf16[32,512]{1,0:T(8,128)(2,1)S(1)}, u32[]{:S(2)}, u32[]{:S(2)}) collective-permute-start(bf16[32,512]{1,0:T(8,128)(2,1)S(1)} %copy.79), channel_id=1, source_target_pairs={{0,8},{8,16},{16,24},{24,32},{32,40},{40,48},{48,56},{56,64},{64,7... | collective-permute-start | bytes 98312 | tf_op jit(solution)/shard_map/while/body/eval_jaxpr/ppermute | solution.py:15
  530.5 8.7 %collective-permute-start.3 = (bf16[32,512]{1,0:T(8,128)(2,1)S(1)}, bf16[32,512]{1,0:T(8,128)(2,1)S(1)}, u32[]{:S(2)}, u32[]{:S(2)}) collective-permute-start(bf16[32,512]{1,0:T(8,128)(2,1)S(1)} %copy.79), channel_id=1, source_target_pairs={{0,8},{8,16},{16,24},{24,32},{32,40},{40,48},{48,56},{56,64},{64,7... | collective-permute-start | bytes 98312 | tf_op jit(solution)/shard_map/while/body/eval_jaxpr/ppermute | solution.py:15
  539.2 8.7 %collective-permute-start.3 = (bf16[32,512]{1,0:T(8,128)(2,1)S(1)}, bf16[32,512]{1,0:T(8,128)(2,1)S(1)}, u32[]{:S(2)}, u32[]{:S(2)}) collective-permute-start(bf16[32,512]{1,0:T(8,128)(2,1)S(1)} %copy.79), channel_id=1, source_target_pairs={{0,8},{8,16},{16,24},{24,32},{32,40},{40,48},{48,56},{56,64},{64,7... | collective-permute-start | bytes 98312 | tf_op jit(solution)/shard_map/while/body/eval_jaxpr/ppermute | solution.py:15
  547.9 8.7 %collective-permute-start.3 = (bf16[32,512]{1,0:T(8,128)(2,1)S(1)}, bf16[32,512]{1,0:T(8,128)(2,1)S(1)}, u32[]{:S(2)}, u32[]{:S(2)}) collective-permute-start(bf16[32,512]{1,0:T(8,128)(2,1)S(1)} %copy.79), channel_id=1, source_target_pairs={{0,8},{8,16},{16,24},{24,32},{32,40},{40,48},{48,56},{56,64},{64,7... | collective-permute-start | bytes 98312 | tf_op jit(solution)/shard_map/while/body/eval_jaxpr/ppermute | solution.py:15
  565.3 8.7 %collective-permute-start.3 = (bf16[32,512]{1,0:T(8,128)(2,1)S(1)}, bf16[32,512]{1,0:T(8,128)(2,1)S(1)}, u32[]{:S(2)}, u32[]{:S(2)}) collective-permute-start(bf16[32,512]{1,0:T(8,128)(2,1)S(1)} %copy.79), channel_id=1, source_target_pairs={{0,8},{8,16},{16,24},{24,32},{32,40},{40,48},{48,56},{56,64},{64,7... | collective-permute-start | bytes 98312 | tf_op jit(solution)/shard_map/while/body/eval_jaxpr/ppermute | solution.py:15
  574.0 8.7 %collective-permute-start.3 = (bf16[32,512]{1,0:T(8,128)(2,1)S(1)}, bf16[32,512]{1,0:T(8,128)(2,1)S(1)}, u32[]{:S(2)}, u32[]{:S(2)}) collective-permute-start(bf16[32,512]{1,0:T(8,128)(2,1)S(1)} %copy.79), channel_id=1, source_target_pairs={{0,8},{8,16},{16,24},{24,32},{32,40},{40,48},{48,56},{56,64},{64,7... | collective-permute-start | bytes 98312 | tf_op jit(solution)/shard_map/while/body/eval_jaxpr/ppermute | solution.py:15
  591.4 8.7 %collective-permute-start.3 = (bf16[32,512]{1,0:T(8,128)(2,1)S(1)}, bf16[32,512]{1,0:T(8,128)(2,1)S(1)}, u32[]{:S(2)}, u32[]{:S(2)}) collective-permute-start(bf16[32,512]{1,0:T(8,128)(2,1)S(1)} %copy.79), channel_id=1, source_target_pairs={{0,8},{8,16},{16,24},{24,32},{32,40},{40,48},{48,56},{56,64},{64,7... | collective-permute-start | bytes 98312 | tf_op jit(solution)/shard_map/while/body/eval_jaxpr/ppermute | solution.py:15
  600.1 8.7 %collective-permute-start.3 = (bf16[32,512]{1,0:T(8,128)(2,1)S(1)}, bf16[32,512]{1,0:T(8,128)(2,1)S(1)}, u32[]{:S(2)}, u32[]{:S(2)}) collective-permute-start(bf16[32,512]{1,0:T(8,128)(2,1)S(1)} %copy.79), channel_id=1, source_target_pairs={{0,8},{8,16},{16,24},{24,32},{32,40},{40,48},{48,56},{56,64},{64,7... | collective-permute-start | bytes 98312 | tf_op jit(solution)/shard_map/while/body/eval_jaxpr/ppermute | solution.py:15
  608.8 8.7 %collective-permute-start.3 = (bf16[32,512]{1,0:T(8,128)(2,1)S(1)}, bf16[32,512]{1,0:T(8,128)(2,1)S(1)}, u32[]{:S(2)}, u32[]{:S(2)}) collective-permute-start(bf16[32,512]{1,0:T(8,128)(2,1)S(1)} %copy.79), channel_id=1, source_target_pairs={{0,8},{8,16},{16,24},{24,32},{32,40},{40,48},{48,56},{56,64},{64,7... | collective-permute-start | bytes 98312 | tf_op jit(solution)/shard_map/while/body/eval_jaxpr/ppermute | solution.py:15
  617.5 8.7 %collective-permute-start.3 = (bf16[32,512]{1,0:T(8,128)(2,1)S(1)}, bf16[32,512]{1,0:T(8,128)(2,1)S(1)}, u32[]{:S(2)}, u32[]{:S(2)}) collective-permute-start(bf16[32,512]{1,0:T(8,128)(2,1)S(1)} %copy.79), channel_id=1, source_target_pairs={{0,8},{8,16},{16,24},{24,32},{32,40},{40,48},{48,56},{56,64},{64,7... | collective-permute-start | bytes 98312 | tf_op jit(solution)/shard_map/while/body/eval_jaxpr/ppermute | solution.py:15
  635.0 8.7 %collective-permute-start.3 = (bf16[32,512]{1,0:T(8,128)(2,1)S(1)}, bf16[32,512]{1,0:T(8,128)(2,1)S(1)}, u32[]{:S(2)}, u32[]{:S(2)}) collective-permute-start(bf16[32,512]{1,0:T(8,128)(2,1)S(1)} %copy.79), channel_id=1, source_target_pairs={{0,8},{8,16},{16,24},{24,32},{32,40},{40,48},{48,56},{56,64},{64,7... | collective-permute-start | bytes 98312 | tf_op jit(solution)/shard_map/while/body/eval_jaxpr/ppermute | solution.py:15
  643.7 8.7 %collective-permute-start.3 = (bf16[32,512]{1,0:T(8,128)(2,1)S(1)}, bf16[32,512]{1,0:T(8,128)(2,1)S(1)}, u32[]{:S(2)}, u32[]{:S(2)}) collective-permute-start(bf16[32,512]{1,0:T(8,128)(2,1)S(1)} %copy.79), channel_id=1, source_target_pairs={{0,8},{8,16},{16,24},{24,32},{32,40},{40,48},{48,56},{56,64},{64,7... | collective-permute-start | bytes 98312 | tf_op jit(solution)/shard_map/while/body/eval_jaxpr/ppermute | solution.py:15
  661.1 8.7 %collective-permute-start.3 = (bf16[32,512]{1,0:T(8,128)(2,1)S(1)}, bf16[32,512]{1,0:T(8,128)(2,1)S(1)}, u32[]{:S(2)}, u32[]{:S(2)}) collective-permute-start(bf16[32,512]{1,0:T(8,128)(2,1)S(1)} %copy.79), channel_id=1, source_target_pairs={{0,8},{8,16},{16,24},{24,32},{32,40},{40,48},{48,56},{56,64},{64,7... | collective-permute-start | bytes 98312 | tf_op jit(solution)/shard_map/while/body/eval_jaxpr/ppermute | solution.py:15
  669.8 8.7 %collective-permute-start.3 = (bf16[32,512]{1,0:T(8,128)(2,1)S(1)}, bf16[32,512]{1,0:T(8,128)(2,1)S(1)}, u32[]{:S(2)}, u32[]{:S(2)}) collective-permute-start(bf16[32,512]{1,0:T(8,128)(2,1)S(1)} %copy.79), channel_id=1, source_target_pairs={{0,8},{8,16},{16,24},{24,32},{32,40},{40,48},{48,56},{56,64},{64,7... | collective-permute-start | bytes 98312 | tf_op jit(solution)/shard_map/while/body/eval_jaxpr/ppermute | solution.py:15
  678.5 8.7 %collective-permute-start.3 = (bf16[32,512]{1,0:T(8,128)(2,1)S(1)}, bf16[32,512]{1,0:T(8,128)(2,1)S(1)}, u32[]{:S(2)}, u32[]{:S(2)}) collective-permute-start(bf16[32,512]{1,0:T(8,128)(2,1)S(1)} %copy.79), channel_id=1, source_target_pairs={{0,8},{8,16},{16,24},{24,32},{32,40},{40,48},{48,56},{56,64},{64,7... | collective-permute-start | bytes 98312 | tf_op jit(solution)/shard_map/while/body/eval_jaxpr/ppermute | solution.py:15
  (189 other events, 1441.1 us)
Sparse Core Ops, SparseCore 0:
  714.2 35.3 reduce-scatter.1
where the time goes:
time: 762 us; the launch traced here: 758 us
  waiting for transfers between devices  442 us (58%)
  blocking collectives  169 us (22%)
  matrix products  50.8 us (7%)
  starting transfers between devices  44.2 us (6%)
  other arithmetic  18.4 us (2%)
  between operations  15 us (2%)
  local copies, waits for them, and re-layouts  12.8 us (2%)
    ppermute x192, waiting for transfers between devices, shifted(): lax.ppermute(array, axis, [(i, (i + by) % length) for i in range(length)])  425 us
    all_gather x1, blocking collectives, body(): every_lse = lax.all_gather(own_lse, 'blk', axis=1, tiled=True)  56.9 us
    all_gather x4, blocking collectives, combined_all(): everything = jax.tree.map(lambda part: lax.all_gather(part, axis), array)  50.1 us
    dot_general x128, matrix products, similarity(): lax.dot_general(left, right, (((1,), (0,)), ((), ())), preferred_element_...  36.1 us
    ppermute x192, starting transfers between devices, shifted(): lax.ppermute(array, axis, [(i, (i + by) % length) for i in range(length)])  33.7 us
    all_gather x1, blocking collectives, body(): lax.all_gather(teacher_image, 'grp', axis=0, tiled=True)  25 us
    all_gather x1, blocking collectives, body(): lax.all_gather(student_image, 'grp', axis=0, tiled=True)  22.1 us
    reduce_scatter x1, waiting for transfers between devices, body(): lax.psum_scatter(image_acc, 'grp', scatter_dimension=0, tiled=True)  17.3 us
  transfers between devices with their start and end apart: 194, of which 65 were waited for; matrix products, arithmetic and copies ran while one was open for 9% of the time, Pallas kernels for 0%

commit v1 on v0

v1 whole, which is shorter than its diff:
```python
import functools
import math

import jax
import jax.numpy as jnp
from jax import lax
from jax.experimental import pallas as pl
from jax.experimental.pallas import tpu as pltpu
from jax.sharding import PartitionSpec as P

MESH = pl.DeviceIdType.MESH
X, Y, Z = 4, 4, 8
PLANE, LINE = X * Y, 2 * Z
ROWS = 32
CHUNK = 128
F32 = jnp.float32
BF16 = jnp.bfloat16


class Place:
    def __init__(self):
        blk = lax.axis_index("blk")
        grp = lax.axis_index("grp")
        self.core = blk % 2
        self.z = (blk // 2) % Z
        self.y = (blk // LINE) * 2 + grp // X
        self.x = grp % X

    def at(self, x=None, y=None, z=None, core=None):
        x = self.x if x is None else x
        y = self.y if y is None else y
        z = self.z if z is None else z
        core = self.core if core is None else core
        return ((y // 2) * LINE + z * 2 + core, (y % 2) * X + x)

    def in_plane(self, slot):
        return self.at(x=slot % X, y=slot // X)

    def in_line(self, slot):
        return self.at(z=slot % Z, core=slot // Z)


def wait_for(ref, sem):
    pltpu.make_async_copy(ref, ref, sem).wait()


def send(src, dst, send_sem, recv_sem, device):
    pltpu.make_async_remote_copy(
        src_ref=src,
        dst_ref=dst,
        send_sem=send_sem,
        recv_sem=recv_sem,
        device_id=device,
        device_id_type=MESH,
    ).start()


class Line:
    def __init__(self, me, buf, send_sem, recv_sem, sib_sem):
        self.me, self.buf, self.ss, self.rs, self.sib = me, buf, send_sem, recv_sem, sib_sem

    def block(self, dz):
        me = self.me
        return self.buf.at[me.core * Z + (me.z + dz + Z) % Z]

    def hop(self, k):
        me = self.me
        up, down = me.at(z=(me.z + 1) % Z), me.at(z=(me.z + Z - 1) % Z)
        if k < 3:
            a, b = self.block(-k), self.block(k)
            send(a, a, self.ss, self.rs.at[2 * k], up)
            send(b, b, self.ss, self.rs.at[2 * k + 1], down)
        else:
            half = ROWS // 2
            a, b = self.block(-k).at[pl.ds(0, half)], self.block(k).at[pl.ds(half, half)]
            send(a, a, self.ss, self.rs.at[6], up)
            send(b, b, self.ss, self.rs.at[6], down)

    def share(self, dz):
        me = self.me
        ref = self.block(dz)
        send(ref, ref, self.ss, self.sib, me.at(core=1 - me.core))

    def begin(self):
        self.hop(0)
        self.share(0)

    def round(self, k):
        if k < 4:
            wait_for(self.block(-k), self.rs.at[2 * (k - 1)])
            wait_for(self.block(k), self.rs.at[2 * (k - 1) + 1])
            self.hop(k)
            self.share(-k)
            self.share(k)
        else:
            wait_for(self.block(4), self.rs.at[6])
            self.share(4)

    def finish(self):
        wait_for(self.buf.at[pl.ds((1 - self.me.core) * Z, Z)], self.sib)


class Sheet:
    def __init__(self, me, buf, first_row, rows, x_first, send_sem, recv_sem):
        self.me, self.buf, self.r0, self.n = me, buf, first_row, rows
        self.x_first, self.ss, self.rs = x_first, send_sem, recv_sem

    def block(self, d1, d2, cols=None):
        me = self.me
        dx, dy = (d1, d2) if self.x_first else (d2, d1)
        slot = ((me.y + dy + Y) % Y) * X + (me.x + dx + X) % X
        rows = pl.ds(self.r0, self.n)
        if cols is None:
            return self.buf.at[slot, rows]
        return self.buf.at[slot, rows, pl.ds(cols * 128, 128)]

    def to(self, axis, by):
        me = self.me
        if (axis == 1) == self.x_first:
            return me.at(x=(me.x + by + X) % X)
        return me.at(y=(me.y + by + Y) % Y)


    ORDER = (0, -1, 1, 2)

    def begin(self):
        ref = self.block(0, 0)
        send(ref, ref, self.ss, self.rs.at[0], self.to(1, 1))
        send(ref, ref, self.ss, self.rs.at[1], self.to(1, -1))

    def second(self, i):
        ref = self.block(self.ORDER[i], 0)
        send(ref, ref, self.ss, self.rs.at[3 + 2 * i], self.to(2, 1))
        send(ref, ref, self.ss, self.rs.at[4 + 2 * i], self.to(2, -1))

    def near(self):
        wait_for(self.block(-1, 0), self.rs.at[0])
        wait_for(self.block(1, 0), self.rs.at[1])
        a, b = self.block(-1, 0, 0), self.block(1, 0, 1)
        send(a, a, self.ss, self.rs.at[2], self.to(1, 1))
        send(b, b, self.ss, self.rs.at[2], self.to(1, -1))
        self.second(1)
        self.second(2)

    def far(self):
        wait_for(self.block(2, 0), self.rs.at[2])
        self.second(3)

    def last(self, i):
        d = self.ORDER[i]
        wait_for(self.block(d, -1), self.rs.at[3 + 2 * i])
        wait_for(self.block(d, 1), self.rs.at[4 + 2 * i])
        a, b = self.block(d, -1, 0), self.block(d, 1, 1)
        send(a, a, self.ss, self.rs.at[11], self.to(2, 1))
        send(b, b, self.ss, self.rs.at[11], self.to(2, -1))

    def finish(self):
        me = self.me
        rows = pl.ds(self.r0, self.n)
        wait_for(self.buf.at[pl.ds(0, 4), rows], self.rs.at[11])


def diagonal():
    rows = lax.broadcasted_iota(jnp.int32, (CHUNK, CHUNK), 0)
    cols = lax.broadcasted_iota(jnp.int32, (CHUNK, CHUNK), 1)
    return rows == cols


def to_lanes(column):
    return jnp.sum(jnp.where(diagonal(), column, 0.0), axis=0, keepdims=True)


def to_rows(lanes):
    return jnp.sum(jnp.where(diagonal(), lanes, 0.0), axis=1, keepdims=True)


def dot(a, b, ca, cb):
    return lax.dot_general(a, b, (((ca,), (cb,)), ((), ())), preferred_element_type=F32)


def across(parts):
    return jnp.concatenate(parts, axis=1)


def kernel(
    stage,
    ti_hbm, tt_hbm, si_hbm, st_hbm,
    image_out, text_out, row_out, col_out,
    tt, st, it, is_, t2, ert, ect, ers, ecs, w, col_max, row_max, row_sum, row_kl,
    msg_l, msg_p, kl_l, kl_p, got_l, got_p, gotk_l, gotk_p,
    tp, tsib, tc, ip, rt, ri,
    local_sem, line_s, line_r, sib_r, plane_s, plane_r,
    small_s, small_r, grad_s, grad_r,
):
    me = Place()
    images = it.shape[0] // 8 * 256
    texts = LINE * ROWS
    teacher, student = tt.shape[2], st.shape[2]
    pairs = float(PLANE * LINE * ROWS)
    mine_p = me.y * X + me.x
    mine_l = me.core * Z + me.z

    own = [
        pltpu.make_async_copy(tt_hbm, tt.at[mine_l], local_sem.at[0]),
        pltpu.make_async_copy(ti_hbm, it.at[mine_p], local_sem.at[1]),
        pltpu.make_async_copy(st_hbm, st.at[mine_l], local_sem.at[2]),
        pltpu.make_async_copy(si_hbm, is_.at[mine_p], local_sem.at[3]),
    ]
    for copy in own:
        copy.start()
    barrier = pltpu.get_barrier_semaphore()

    def greet(d, carry):
        pl.semaphore_signal(barrier, inc=1, device_id=me.in_line((mine_l + d) % LINE), device_id_type=MESH)
        pl.semaphore_signal(barrier, inc=1, device_id=me.in_plane((mine_p + d) % PLANE), device_id_type=MESH)
        return carry

    lax.fori_loop(1, 16, greet, 0)
    for copy in own:
        copy.wait()
    pl.semaphore_wait(barrier, 30)

    lines = [Line(me, buf, line_s.at[n], line_r.at[n], sib_r.at[n]) for n, buf in enumerate((tt, st))]
    sheets = []
    for n, buf in enumerate((it, is_)):
        half = buf.shape[1] // 2
        sheets.append(
            [
                Sheet(me, buf, 0, half, True, plane_s.at[n], plane_r.at[2 * n]),
                Sheet(me, buf, half, half, False, plane_s.at[n], plane_r.at[2 * n + 1]),
            ]
        )
    for n in range(2):
        lines[n].begin()
        for sheet in sheets[n]:
            sheet.begin()
        for sheet in sheets[n]:
            sheet.second(0)
    for n in range(2):
        lines[n].round(1)
        for sheet in sheets[n]:
            sheet.near()
        for sheet in sheets[n]:
            sheet.last(0)
    for n in range(2):
        lines[n].round(2)
        for sheet in sheets[n]:
            sheet.far()
        for i in (1, 2):
            for sheet in sheets[n]:
                sheet.last(i)
    for n in range(2):
        lines[n].round(3)
        for sheet in sheets[n]:
            sheet.last(3)
    for n in range(2):
        lines[n].round(4)
        for sheet in sheets[n]:
            sheet.finish()
        lines[n].finish()

    if stage >= 2:
        blocks = images // 256
        keep = 256 // ROWS
        scale_t = math.log2(math.e) / math.sqrt(teacher)
        scale_s = math.log2(math.e) / math.sqrt(student)
        cut = CHUNK // ROWS

        def logits(k, carry):
            rows = pl.ds(pl.multiple_of(k * CHUNK, CHUNK), CHUNK)
            mine = pl.ds(k * cut, cut)
            for which in range(2):
                src, img, er, ec = ((tt, it, ert, ect), (st, is_, ers, ecs))[which]
                width = src.shape[2]
                block = src[mine].reshape(CHUNK, width)
                scale = (scale_t, scale_s)[which]
                tiles = [
                    dot(block, img[pl.ds(a * keep, keep)].reshape(width, 256), 1, 0) * scale for a in range(blocks)
                ]
                top = jnp.max(functools.reduce(jnp.maximum, tiles), axis=1, keepdims=True)
                col_max[which, rows] = top
                col_parts = []
                kl_parts = []
                gaps = []
                for a in range(blocks):
                    cols = pl.ds(a * 256, 256)
                    e_col = jnp.exp2(tiles[a] - top)
                    ec[rows, cols] = e_col
                    col_parts.append(e_col)
                    high = jnp.max(tiles[a], axis=0, keepdims=True)
                    e_row = jnp.exp2(tiles[a] - high)
                    er[rows, cols] = e_row
                    row_max[which, pl.ds(k, 1), cols] = high
                    row_sum[which, pl.ds(k, 1), cols] = jnp.sum(e_row, axis=0, keepdims=True)
                    if which == 0:
                        t2[rows, cols] = tiles[a]
                    else:
                        gap = t2[rows, cols] - tiles[a]
                        kl_parts.append(ect[rows, cols] * gap)
                        row_kl[pl.ds(k, 1), cols] = jnp.sum(ert[rows, cols] * gap, axis=0, keepdims=True)
                total = jnp.sum(functools.reduce(jnp.add, col_parts), axis=1, keepdims=True)
                msg_l[pl.ds(4 * which + k, 1), :] = to_lanes(top + jnp.log2(total))
                if which == 0:
                    total_t = total
                else:
                    kl = jnp.sum(functools.reduce(jnp.add, kl_parts), axis=1, keepdims=True)
                    kl_l[pl.ds(k, 1), :] = to_lanes(kl / total_t)
            return carry

        kl_l[...] = jnp.zeros_like(kl_l)
        kl_p[...] = jnp.zeros_like(kl_p)
        lax.fori_loop(0, texts // CHUNK, logits, 0)
        for which in range(2):
            high = row_max[which]
            top = jnp.max(high, axis=0, keepdims=True)
            part = jnp.exp2(high - top)
            total = jnp.sum(row_sum[which] * part, axis=0, keepdims=True)
            lse = top + jnp.log2(total)
            for a in range(4):
                msg_p[4 * which + a : 4 * which + a + 1, :] = lse[:, a * 128 : a * 128 + 128]
            if which == 0:
                kl = jnp.sum(row_kl[...] * part, axis=0, keepdims=True) / total
                for a in range(4):
                    kl_p[a : a + 1, :] = kl[:, a * 128 : a * 128 + 128]

    if stage >= 3:
        groups = ((msg_p, kl_p, got_p, gotk_p, me.in_plane, mine_p), (msg_l, kl_l, got_l, gotk_l, me.in_line, mine_l))
        for n in range(2):

            def tell(d, carry):
                for g, (msg, kl, got, gotk, where, mine) in enumerate(groups):
                    src, dst = ((msg, got), (kl, gotk))[n]
                    send(src, dst.at[d], small_s.at[n, g], small_r.at[n, g], where((mine + d) % 16))
                return carry

            lax.fori_loop(1, 16, tell, 0)
        lse = []
        for g, (msg, kl, got, gotk, where, mine) in enumerate(groups):
            got[0] = msg[...]
            wait_for(got.at[pl.ds(1, 15)], small_r.at[0, g])
            every = got[...]
            top = jnp.max(every, axis=0)
            lse.append(top + jnp.log2(jnp.sum(jnp.exp2(every - top[None]), axis=0)))

    if stage >= 4:
        image_lse = [across([lse[0][4 * which + a : 4 * which + a + 1, :] for a in range(4)]) for which in range(2)]
        got_l[0] = lse[1]
        half_slots = Z

        def weigh(n, carry):
            k = ((1 - me.core) * 2 + n) % 4
            rows = pl.ds(pl.multiple_of(k * CHUNK, CHUNK), CHUNK)
            factors = []
            for which in range(2):
                by_row = jnp.exp2(row_max[which, pl.ds(k, 1), :] - image_lse[which]) * pairs
                col_lse = to_rows(got_l[0, pl.ds(4 * which + k, 1), :])
                by_col = jnp.exp2(col_max[which, rows] - col_lse) * pairs
                factors.append((by_row, by_col))
            (row_t, col_t), (row_s, col_s) = factors
            total = None
            for a in range(images // 256):
                cols = pl.ds(a * 256, 256)
                lanes = slice(a * 256, a * 256 + 256)
                weights = (
                    ers[rows, cols] * row_s[:, lanes]
                    - ert[rows, cols] * row_t[:, lanes]
                    + ecs[rows, cols] * col_s
                    - ect[rows, cols] * col_t
                ).astype(BF16)
                w[rows, cols] = weights
                part = dot(weights, is_[pl.ds(a * 8, 8)].reshape(student, 256), 1, 1)
                total = part if total is None else total + part
            tp[pl.ds(k * 4, 4)] = total.astype(BF16).reshape(4, ROWS, student)
            return carry

        other = pl.ds((1 - me.core) * Z, Z)
        lax.fori_loop(0, 2, weigh, 0)
        send(tp.at[other], tsib, grad_s.at[0], grad_r.at[0], me.at(core=1 - me.core))
        lax.fori_loop(2, 4, weigh, 0)

        texts_s = st[...].reshape(texts, student)
        for a in range(images // CHUNK):
            part = dot(w[:, a * CHUNK : (a + 1) * CHUNK], texts_s, 0, 0)
            ip[a * 4 : a * 4 + 4] = part.astype(BF16).reshape(4, ROWS, student)

        def give_plane(d, carry):
            slot = (mine_p + d) % PLANE
            send(ip.at[slot], ri.at[d], grad_s.at[1], grad_r.at[1], me.in_plane(slot))
            return carry

        lax.fori_loop(1, PLANE, give_plane, 0)
        wait_for(tsib, grad_r.at[0])
        tc[...] = (tp[pl.ds(me.core * Z, Z)].astype(F32) + tsib[...].astype(F32)).astype(BF16)

        def give_line(d, carry):
            z = (me.z + d) % Z
            send(tc.at[z], rt.at[d], grad_s.at[2], grad_r.at[2], me.at(z=z))
            return carry

        lax.fori_loop(1, Z, give_line, 0)

        for g, (msg, kl, got, gotk, where, mine) in enumerate(groups):
            got[0] = msg[...]
            gotk[0] = kl[...]
            wait_for(gotk.at[pl.ds(1, 15)], small_r.at[1, g])
            share = jnp.exp2(got[:, 0:4, :] - lse[g][None, 0:4, :])
            kl_sum = jnp.sum(gotk[:, 0:4, :] * share, axis=0)
            loss = (kl_sum - lse[g][0:4] + lse[g][4:8]) * math.log(2.0)
            out = (row_out, col_out)[g]
            out[...] = jnp.concatenate([loss, loss], axis=0)

        ri[0] = ip[mine_p]
        rt[0] = tc[me.z]
        wait_for(ri.at[pl.ds(1, 15)], grad_r.at[1])
        image_out[...] = jnp.sum(ri[...].astype(F32), axis=0)
        wait_for(rt.at[pl.ds(1, 7)], grad_r.at[2])
        text_out[...] = jnp.sum(rt[...].astype(F32), axis=0)
        wait_for(tsib, grad_s.at[0])
        wait_for(ri.at[pl.ds(1, 15)], grad_s.at[1])
        wait_for(rt.at[pl.ds(1, 7)], grad_s.at[2])

    if stage >= 3:
        for g, (msg, kl, got, gotk, where, mine) in enumerate(groups):
            if stage == 3:
                wait_for(gotk.at[pl.ds(1, 15)], small_r.at[1, g])
            wait_for(got.at[pl.ds(1, 15)], small_s.at[0, g])
            wait_for(gotk.at[pl.ds(1, 15)], small_s.at[1, g])
    for n, (texts_buf, image_buf) in enumerate(((tt, it), (st, is_))):
        wait_for(texts_buf.at[pl.ds(0, 15)], line_s.at[n])
        wait_for(image_buf.at[pl.ds(0, 15)], plane_s.at[n])


def body(teacher_image, teacher_text, student_image, student_text, stage=4):
    teacher, student = teacher_text.shape[1], student_text.shape[1]
    texts, images = LINE * ROWS, PLANE * ROWS
    chunks = texts // CHUNK
    vmem = pltpu.VMEM
    dma = pltpu.SemaphoreType.DMA
    outs = pl.pallas_call(
        functools.partial(kernel, stage),
        out_shape=(
            jax.ShapeDtypeStruct((ROWS, student), F32),
            jax.ShapeDtypeStruct((ROWS, student), F32),
            jax.ShapeDtypeStruct((8, 128), F32),
            jax.ShapeDtypeStruct((8, 128), F32),
        ),
        in_specs=[pl.BlockSpec(memory_space=pl.ANY)] * 4,
        out_specs=(pl.BlockSpec(memory_space=pltpu.VMEM),) * 4,
        scratch_shapes=[
            vmem((LINE, ROWS, teacher), BF16),
            vmem((LINE, ROWS, student), BF16),
            vmem((PLANE,) + teacher_image.shape, BF16),
            vmem((PLANE,) + student_image.shape, BF16),
            vmem((texts, images), F32),
            vmem((texts, images), F32),
            vmem((texts, images), F32),
            vmem((texts, images), F32),
            vmem((texts, images), F32),
            vmem((texts, images), BF16),
            vmem((2, texts, 1), F32),
            vmem((2, chunks, images), F32),
            vmem((2, chunks, images), F32),
            vmem((chunks, images), F32),
            vmem((8, 128), F32),
            vmem((8, 128), F32),
            vmem((8, 128), F32),
            vmem((8, 128), F32),
            vmem((16, 8, 128), F32),
            vmem((16, 8, 128), F32),
            vmem((16, 8, 128), F32),
            vmem((16, 8, 128), F32),
            vmem((LINE, ROWS, student), BF16),
            vmem((Z, ROWS, student), BF16),
            vmem((Z, ROWS, student), BF16),
            vmem((PLANE, ROWS, student), BF16),
            vmem((Z, ROWS, student), BF16),
            vmem((PLANE, ROWS, student), BF16),
            dma((4,)),
            dma((2,)),
            dma((2, 7)),
            dma((2,)),
            dma((2,)),
            dma((4, 12)),
            dma((2, 2)),
            dma((2, 2)),
            dma((3,)),
            dma((3,)),
        ],
        compiler_params=pltpu.CompilerParams(
            collective_id=0, has_side_effects=True, vmem_limit_bytes=48 * 1024 * 1024
        ),
        name="distill",
    )(teacher_image, teacher_text, student_image, student_text)
    image_sum, text_sum, row_tile, col_tile = outs
    blk, grp = lax.axis_index("blk"), lax.axis_index("grp")
    scale = 1.0 / math.sqrt(student)
    slot_p = (blk // LINE) * 8 + grp
    slot_l = (blk % 2) * Z + (blk // 2) % Z
    row_loss = lax.dynamic_slice(row_tile.reshape(8 * 128), (slot_p * ROWS,), (ROWS,))
    column_loss = lax.dynamic_slice(col_tile.reshape(8 * 128), (slot_l * ROWS,), (ROWS,))
    return (image_sum * scale, text_sum * scale, row_loss, column_loss)


def solution(mesh):
    in_specs = (P("grp", "blk"), P(("blk", "grp"), None), P("grp", "blk"), P(("blk", "grp"), None))
    out_specs = (
        P(("blk", "grp"), None),
        P(("blk", "grp"), None),
        P(("blk", "grp")),
        P(("blk", "grp")),
    )
    return jax.shard_map(body, mesh=mesh, in_specs=in_specs, out_specs=out_specs, check_vma=False)
```

time: 762 us -> 55.4 us (0.07)
  waiting for transfers between devices: 442 us -> 0 us
  blocking collectives: 169 us -> 0 us
  matrix products: 50.8 us -> 0 us
  Pallas kernels: 0 us -> 49.3 us
  starting transfers between devices: 44.2 us -> 0 us
  other arithmetic: 18.4 us -> 0.66 us
  between operations: 15 us -> 0.71 us
  local copies, waits for them, and re-layouts: 12.8 us -> 4.4 us
    ppermute x192 -> x0, waiting for transfers between devices: 425 us -> none  [shifted(): lax.ppermute(array, axis, [(i, (i + by) % length) for i in range(length)])]
    all_gather x7 -> x0, blocking collectives: 154 us -> none  [the longest x1 56.9 us: body(): every_lse = lax.all_gather(own_lse, 'blk', axis=1, tiled=True)]
    dot_general x192 -> x0, matrix products: 50.8 us -> none  [the longest x128 36.1 us: similarity(): lax.dot_general(left, right, (((1,), (0,)), ((), ())), preferred_element_...]
    pallas_call x0 -> x1, Pallas kernels: none -> 49.3 us  [body(): pl.pallas_call(functools.partial(kernel, stage), out_shape=(jax.ShapeDtyp...]
    ppermute x192 -> x0, starting transfers between devices: 33.7 us -> none  [shifted(): lax.ppermute(array, axis, [(i, (i + by) % length) for i in range(length)])]
    reduce_scatter x1 -> x0, waiting for transfers between devices: 17.3 us -> none  [body(): lax.psum_scatter(image_acc, 'grp', scatter_dimension=0, tiled=True)]
    unnamed x1 -> x0, blocking collectives: 14.6 us -> none
    reduce_sum x66 -> x0, other arithmetic: 12.2 us -> none  [the longest x64 12.1 us: tile_stats(): jnp.sum(jnp.exp(logits - jnp.expand_dims(highest, axis)), axis=axis)]
  transfers between devices with their start and end apart: 194 -> 0, of which waited for: 65 -> 0; matrix products, arithmetic and copies ran while one was open for 9% -> 0% of each run, Pallas kernels for 0% -> 0%
where the time goes in v1:
time: 55.4 us; the launch traced here: 55.1 us
  Pallas kernels  49.3 us (89%)
  local copies, waits for them, and re-layouts  4.4 us (8%)
  between operations  0.71 us (1%)
  other arithmetic  0.66 us (1%)
    pallas_call x1, Pallas kernels, body(): pl.pallas_call(functools.partial(kernel, stage), out_shape=(jax.ShapeDtyp...  49.3 us
    unnamed x8, local copies, waits for them, and re-layouts  3.23 us

profile of v1, /device:TPU:1, one launch (start us, length us, event | category | flops | bytes accessed | tf_op | source)
XLA Modules:
  0.0 55.1 jit_solution(4564942171237173533)
XLA Ops:
  0.6 0.0 copy-start
  0.7 0.8 %copy-done = bf16[160,256]{1,0:T(8,128)(2,1)S(1)} copy-done((bf16[160,256]{1,0:T(8,128)(2,1)S(1)}, bf16[160,256]{1,0:T(8,128)(2,1)}, u32[]{:S(2)}) %copy-start) | copy-done | bytes 81944
  1.5 0.0 copy-start.1
  1.5 0.9 %copy-done.1 = bf16[32,1280]{1,0:T(8,128)(2,1)S(1)} copy-done((bf16[32,1280]{1,0:T(8,128)(2,1)S(1)}, bf16[32,1280]{1,0:T(8,128)(2,1)}, u32[]{:S(2)}) %copy-start.1) | copy-done | bytes 81944
  2.4 0.0 copy-start.2
  2.4 0.8 %copy-done.2 = bf16[64,256]{1,0:T(8,128)(2,1)S(1)} copy-done((bf16[64,256]{1,0:T(8,128)(2,1)S(1)}, bf16[64,256]{1,0:T(8,128)(2,1)}, u32[]{:S(2)}) %copy-start.2) | copy-done | bytes 32792
  3.2 0.0 copy-start.3
  3.2 0.8 %copy-done.3 = bf16[32,512]{1,0:T(8,128)(2,1)S(1)} copy-done((bf16[32,512]{1,0:T(8,128)(2,1)S(1)}, bf16[32,512]{1,0:T(8,128)(2,1)}, u32[]{:S(2)}) %copy-start.3) | copy-done | bytes 32792
  3.9 49.3 %distill.1 = (f32[32,512]{1,0:T(8,128)S(1)}, f32[32,512]{1,0:T(8,128)S(1)}, f32[8,128]{1,0:T(8,128)S(1)}, f32[8,128]{1,0:T(8,128)S(1)}) custom-call(bf16[160,256]{1,0:T(8,128)(2,1)S(1)} %copy-done, bf16[32,1280]{1,0:T(8,128)(2,1)S(1)} %copy-done.1, bf16[64,256]{1,0:T(8,128)(2,1)S(1)} %copy-done.2, bf16[32,512]{1,0:T(8,128)(2,1)S(1)} %copy-done.3), custom_call_target="tpu_custom_call" | custom-call | tf_op jit(solution)/shard_map/distill/pallas_call | solution.py:439
  53.3 0.6 %dynamic_slice.7 = f32[32]{0:T(128)} dynamic-slice(f32[1024]{0:T(1024)S(1)} %bitcast.3, s32[]{:T(128)S(6)} %select_n.29), dynamic_slice_sizes={32} | dynamic-slice | bytes 260 | tf_op jit(solution)/shard_map/dynamic_slice | solution.py:500
  53.8 0.6 %dynamic_slice.6 = f32[32]{0:T(128)} dynamic-slice(f32[1024]{0:T(1024)S(1)} %bitcast.2, s32[]{:T(128)S(6)} %select_n.25), dynamic_slice_sizes={32} | dynamic-slice | bytes 260 | tf_op jit(solution)/shard_map/dynamic_slice | solution.py:499
  54.4 0.7 %broadcast_multiply_fusion = (f32[32,512]{1,0:T(8,128)}, f32[32,512]{1,0:T(8,128)}) fusion(f32[32,512]{1,0:T(8,128)S(1)} %get-tuple-element.9, f32[32,512]{1,0:T(8,128)S(1)} %get-tuple-element.8), kind=kLoop, calls=%fused_computation | loop fusion | flops 32768 | bytes 262144 | tf_op jit(solution)/shard_map/mul | solution.py:501
Async XLA Ops:
  0.6 0.9 %copy-start = (bf16[160,256]{1,0:T(8,128)(2,1)S(1)}, bf16[160,256]{1,0:T(8,128)(2,1)}, u32[]{:S(2)}) copy-start(bf16[160,256]{1,0:T(8,128)(2,1)} %ti_hbm.1) | copy-start | bytes 245764
  1.5 0.9 %copy-start.1 = (bf16[32,1280]{1,0:T(8,128)(2,1)S(1)}, bf16[32,1280]{1,0:T(8,128)(2,1)}, u32[]{:S(2)}) copy-start(bf16[32,1280]{1,0:T(8,128)(2,1)} %tt_hbm.1) | copy-start | bytes 245764
  2.4 0.8 %copy-start.2 = (bf16[64,256]{1,0:T(8,128)(2,1)S(1)}, bf16[64,256]{1,0:T(8,128)(2,1)}, u32[]{:S(2)}) copy-start(bf16[64,256]{1,0:T(8,128)(2,1)} %si_hbm.1) | copy-start | bytes 98308
  3.2 0.8 %copy-start.3 = (bf16[32,512]{1,0:T(8,128)(2,1)S(1)}, bf16[32,512]{1,0:T(8,128)(2,1)}, u32[]{:S(2)}) copy-start(bf16[32,512]{1,0:T(8,128)(2,1)} %st_hbm.1) | copy-start | bytes 98308

commit v2 on v0

v2 whole, which is shorter than its diff:
```python
import functools
import math

import jax
import jax.numpy as jnp
from jax import lax
from jax.experimental import pallas as pl
from jax.experimental.pallas import tpu as pltpu
from jax.sharding import PartitionSpec as P

MESH = pl.DeviceIdType.MESH
X, Y, Z = 4, 4, 8
PLANE, LINE = X * Y, 2 * Z
ROWS = 32
CHUNK = 128
F32 = jnp.float32
BF16 = jnp.bfloat16


class Place:
    def __init__(self):
        blk = lax.axis_index("blk")
        grp = lax.axis_index("grp")
        self.core = blk % 2
        self.z = (blk // 2) % Z
        self.y = (blk // LINE) * 2 + grp // X
        self.x = grp % X

    def at(self, x=None, y=None, z=None, core=None):
        x = self.x if x is None else x
        y = self.y if y is None else y
        z = self.z if z is None else z
        core = self.core if core is None else core
        return ((y // 2) * LINE + z * 2 + core, (y % 2) * X + x)

    def in_plane(self, slot):
        return self.at(x=slot % X, y=slot // X)

    def in_line(self, slot):
        return self.at(z=slot % Z, core=slot // Z)


def wait_for(ref, sem):
    pltpu.make_async_copy(ref, ref, sem).wait()


def send(src, dst, send_sem, recv_sem, device):
    pltpu.make_async_remote_copy(
        src_ref=src,
        dst_ref=dst,
        send_sem=send_sem,
        recv_sem=recv_sem,
        device_id=device,
        device_id_type=MESH,
    ).start()


class Gather:
    NEAR = (2, -1, 1)

    def __init__(self, me, texts, images, send_sem, line_r, plane_r, other_r):
        self.me, self.texts, self.images = me, texts, images
        self.ss, self.line_r, self.plane_r, self.other = send_sem, line_r, plane_r, other_r

    def text(self, dz):
        me = self.me
        return self.texts.at[me.core * Z + lax.rem(me.z + dz + Z, Z)]

    def image(self, dx, dy):
        me = self.me
        return self.images.at[lax.rem(me.y + dy + Y, Y) * X + lax.rem(me.x + dx + X, X)]

    def up(self, ref, sem, by):
        me = self.me
        send(ref, ref, self.ss.at[0], self.line_r.at[sem], me.at(z=lax.rem(me.z + by + Z, Z)))

    def share(self, dz):
        ref = self.text(dz)
        send(ref, ref, self.ss.at[0], self.other, self.me.at(core=1 - self.me.core))

    def over(self, ref, sem, axis, by):
        me = self.me
        if axis == 0:
            to = me.at(x=lax.rem(me.x + by + X, X))
        else:
            to = me.at(y=lax.rem(me.y + by + Y, Y))
        send(ref, ref, self.ss.at[1], self.plane_r.at[sem], to)

    def plane_begin(self):
        own = self.image(0, 0)
        for n, by in enumerate((2, 1, -1)):
            self.over(own, n, 0, by)
            self.over(own, 3 + n, 1, by)

    def line_far(self):
        own = self.text(0)
        self.up(own, 0, 2)
        self.up(own, 1, -2)

    def line_near(self):
        own = self.text(0)
        self.up(own, 2, 1)
        self.up(own, 3, -1)
        self.share(0)

    def plane_turn(self):
        rows = self.images.shape[1] // 2
        for n, by in enumerate(self.NEAR):
            for axis in range(2):
                block = self.image(by, 0) if axis == 0 else self.image(0, by)
                wait_for(block, self.plane_r.at[3 * axis + n])
                part = block.at[pl.ds(axis * rows, rows)]
                for to in (2, 1, -1):
                    self.over(part, 6, 1 - axis, to)

    def line_turn(self):
        half = ROWS // 2
        a, b = self.text(-2), self.text(2)
        wait_for(a, self.line_r.at[0])
        wait_for(b, self.line_r.at[1])
        self.up(a.at[pl.ds(0, half)], 6, 2)
        self.up(b.at[pl.ds(half, half)], 6, -2)
        self.up(a, 4, 1)
        self.up(b, 5, -1)
        self.share(-2)
        self.share(2)
        wait_for(self.text(-1), self.line_r.at[2])
        wait_for(self.text(1), self.line_r.at[3])
        self.share(-1)
        self.share(1)

    def line_finish(self):
        wait_for(self.text(-3), self.line_r.at[4])
        wait_for(self.text(3), self.line_r.at[5])
        self.share(-3)
        self.share(3)
        wait_for(self.text(4), self.line_r.at[6])
        self.share(4)

    def finish(self):
        wait_for(self.images.at[pl.ds(0, 9)], self.plane_r.at[6])
        wait_for(self.texts.at[pl.ds((1 - self.me.core) * Z, Z)], self.other)

    def end(self):
        wait_for(self.texts.at[pl.ds(0, 15)], self.ss.at[0])
        wait_for(self.images.at[pl.ds(0, 15)], self.ss.at[1])


def diagonal():
    rows = lax.broadcasted_iota(jnp.int32, (CHUNK, CHUNK), 0)
    cols = lax.broadcasted_iota(jnp.int32, (CHUNK, CHUNK), 1)
    return rows == cols


def to_lanes(column):
    return jnp.sum(jnp.where(diagonal(), column, 0.0), axis=0, keepdims=True)


def to_rows(lanes):
    return jnp.sum(jnp.where(diagonal(), lanes, 0.0), axis=1, keepdims=True)


def dot(a, b, ca, cb):
    return lax.dot_general(a, b, (((ca,), (cb,)), ((), ())), preferred_element_type=F32)


def across(parts):
    return jnp.concatenate(parts, axis=1)


def kernel(
    stage,
    ti_hbm, tt_hbm, si_hbm, st_hbm,
    image_out, text_out, row_out, col_out,
    tt, st, it, is_, s2, ert, ect, ers, ecs, w, col_max, row_max, row_sum, row_kl,
    s_line, s_plane, t_line, t_plane, gs_line, gs_plane, gt_line, gt_plane, col_lse,
    tp, tsend, tsib, tc, ip, rt, ri,
    local_sem, gather_sem, line_r, plane_r, other_r,
    small_s, small_r, sib_s, sib_r, grad_s, grad_r,
):
    me = Place()
    texts, images = LINE * ROWS, PLANE * ROWS
    teacher, student = tt.shape[2], st.shape[2]
    pairs = float(images * LINE)
    chunks = texts // CHUNK
    cut = CHUNK // ROWS
    mine_p = me.y * X + me.x
    mine_l = me.core * Z + me.z

    own = [
        pltpu.make_async_copy(tt_hbm, tt.at[mine_l], local_sem.at[0]),
        pltpu.make_async_copy(ti_hbm, it.at[mine_p], local_sem.at[1]),
        pltpu.make_async_copy(st_hbm, st.at[mine_l], local_sem.at[2]),
        pltpu.make_async_copy(si_hbm, is_.at[mine_p], local_sem.at[3]),
    ]
    for copy in own:
        copy.start()
    barrier = pltpu.get_barrier_semaphore()

    near = [me.at(core=1 - me.core)]
    near += [me.at(z=lax.rem(me.z + dz, Z)) for dz in (1, 2, Z - 2, Z - 1)]
    near += [me.at(x=lax.rem(me.x + d, X)) for d in range(1, X)]
    near += [me.at(y=lax.rem(me.y + d, Y)) for d in range(1, Y)]
    for device in near:
        pl.semaphore_signal(barrier, inc=1, device_id=device, device_id_type=MESH)
    for copy in own:
        copy.wait()
    pl.semaphore_wait(barrier, len(near))

    teacher_in = Gather(me, tt, it, gather_sem.at[0], line_r.at[0], plane_r.at[0], other_r.at[0])
    student_in = Gather(me, st, is_, gather_sem.at[1], line_r.at[1], plane_r.at[1], other_r.at[1])
    both = (student_in, teacher_in)
    for g in both:
        g.line_far()
        g.plane_begin()
    for g in both:
        g.line_near()
    for g in both:
        g.plane_turn()
        g.line_turn()

    def tiles_of(k, texts_buf, image_buf):
        width = texts_buf.shape[2]
        scale = math.log2(math.e) / math.sqrt(width)
        block = texts_buf[pl.ds(k * cut, cut)].reshape(CHUNK, width)
        return [dot(block, image_buf[pl.ds(a * 8, 8)].reshape(width, 256), 1, 0) * scale for a in range(images // 256)]

    def stats(k, which, tiles, er, ec, seen):
        rows = pl.ds(pl.multiple_of(k * CHUNK, CHUNK), CHUNK)
        top = jnp.max(functools.reduce(jnp.maximum, tiles), axis=1, keepdims=True)
        col_max[which, rows] = top
        sums = []
        for a, tile in enumerate(tiles):
            cols = pl.ds(a * 256, 256)
            e_col = jnp.exp2(tile - top)
            ec[rows, cols] = e_col
            sums.append(e_col)
            high = jnp.max(tile, axis=0, keepdims=True)
            e_row = jnp.exp2(tile - high)
            er[rows, cols] = e_row
            row_max[which, pl.ds(k, 1), cols] = high
            row_sum[which, pl.ds(k, 1), cols] = jnp.sum(e_row, axis=0, keepdims=True)
            seen(rows, cols, tile, e_row, e_col)
        total = jnp.sum(functools.reduce(jnp.add, sums), axis=1, keepdims=True)
        return top + jnp.log2(total), total

    def row_stats(which):
        high = row_max[which]
        top = jnp.max(high, axis=0, keepdims=True)
        part = jnp.exp2(high - top)
        total = jnp.sum(row_sum[which] * part, axis=0, keepdims=True)
        return top + jnp.log2(total), part, total

    def lay(ref, first, lanes):
        for a in range(4):
            ref[first + a : first + a + 1, :] = lanes[:, a * 128 : a * 128 + 128]

    groups = (me.in_plane, mine_p, (s_plane, gs_plane), (t_plane, gt_plane)), (
        me.in_line, mine_l, (s_line, gs_line), (t_line, gt_line))

    def tell(n):
        def one(d, carry):
            for g, (where, mine, *pair) in enumerate(groups):
                msg, got = pair[n]
                send(msg, got.at[d], small_s.at[n, g], small_r.at[n, g], where((mine + d) % 16))
            return carry

        lax.fori_loop(1, 16, one, 0)

    def hear(n, g):
        msg, got = groups[g][2 + n]
        got[0] = msg[...]
        wait_for(got.at[pl.ds(1, 15)], small_r.at[n, g])
        every = got[:, 0:4, :]
        top = jnp.max(every, axis=0)
        return top + jnp.log2(jnp.sum(jnp.exp2(every - top[None]), axis=0))

    student_in.line_finish()
    student_in.finish()
    if stage >= 2:

        def student_chunk(k, carry):
            tiles = tiles_of(k, st, is_)

            def seen(rows, cols, tile, e_row, e_col):
                s2[rows, cols] = tile

            lse, _ = stats(k, 1, tiles, ers, ecs, seen)
            s_line[pl.ds(k, 1), :] = to_lanes(lse)
            return carry

        lax.fori_loop(0, chunks, student_chunk, 0)
        lay(s_plane, 0, row_stats(1)[0])
    if stage >= 3:
        tell(0)
    teacher_in.line_finish()
    teacher_in.finish()
    if stage >= 2:

        def teacher_chunk(k, carry):
            tiles = tiles_of(k, tt, it)
            kls = []

            def seen(rows, cols, tile, e_row, e_col):
                gap = tile - s2[rows, cols]
                kls.append(e_col * gap)
                row_kl[pl.ds(k, 1), cols] = jnp.sum(e_row * gap, axis=0, keepdims=True)

            lse, total = stats(k, 0, tiles, ert, ect, seen)
            t_line[pl.ds(k, 1), :] = to_lanes(lse)
            kl = jnp.sum(functools.reduce(jnp.add, kls), axis=1, keepdims=True)
            t_line[pl.ds(4 + k, 1), :] = to_lanes(kl / total)
            return carry

        lax.fori_loop(0, chunks, teacher_chunk, 0)
        lse, part, total = row_stats(0)
        lay(t_plane, 0, lse)
        lay(t_plane, 4, jnp.sum(row_kl[...] * part, axis=0, keepdims=True) / total)
    if stage >= 3:
        tell(1)
        lse_s = [hear(0, 0), hear(0, 1)]
        if stage >= 4:
            image_lse = across([lse_s[0][a : a + 1, :] for a in range(4)])
            col_lse[...] = lse_s[1]

            def student_part(k, carry):
                rows = pl.ds(pl.multiple_of(k * CHUNK, CHUNK), CHUNK)
                by_row = jnp.exp2(row_max[1, pl.ds(k, 1), :] - image_lse) * pairs
                by_col = jnp.exp2(col_max[1, rows] - to_rows(col_lse[pl.ds(k, 1), :])) * pairs
                ers[rows, :] = ers[rows, :] * by_row + ecs[rows, :] * by_col
                return carry

            lax.fori_loop(0, chunks, student_part, 0)
        lse_t = [hear(1, 0), hear(1, 1)]

    if stage >= 4:
        image_lse = across([lse_t[0][a : a + 1, :] for a in range(4)])
        col_lse[...] = lse_t[1]
        other = 1 - me.core

        def weigh(k):
            rows = pl.ds(pl.multiple_of(k * CHUNK, CHUNK), CHUNK)
            by_row = jnp.exp2(row_max[0, pl.ds(k, 1), :] - image_lse) * pairs
            by_col = jnp.exp2(col_max[0, rows] - to_rows(col_lse[pl.ds(k, 1), :])) * pairs
            weights = (ers[rows, :] - ert[rows, :] * by_row - ect[rows, :] * by_col).astype(BF16)
            w[rows, :] = weights
            parts = [
                dot(weights[:, a * 256 : a * 256 + 256], is_[pl.ds(a * 8, 8)].reshape(student, 256), 1, 1)
                for a in range(images // 256)
            ]
            return functools.reduce(jnp.add, parts).reshape(cut, ROWS, student)

        half = lax.div(me.z, 4)

        def part_of(n):
            h = lax.rem(half + 1 + n, 2)
            return h, pl.ds(h * cut, cut)

        for n in range(2):
            h, part = part_of(n)
            tsend[part] = weigh(other * 2 + h).astype(BF16)
            send(tsend.at[part], tsib.at[part], sib_s.at[n], sib_r.at[n], me.at(core=other))
        for n in range(2):
            h, part = part_of(n)
            tp[part] = weigh(me.core * 2 + h)

        def give_line(n):
            h, part = part_of(n)
            wait_for(tsib.at[part], sib_r.at[n])
            tc[part] = (tp[part] + tsib[part].astype(F32)).astype(BF16)
            for i in range(n, 4):
                z = h * 4 + lax.rem(me.z + i, 4)
                d = lax.rem(z - me.z + Z, Z)
                send(tc.at[z], rt.at[d], grad_s.at[1], grad_r.at[1], me.at(z=z))

        def give_plane(dy):
            y = lax.rem(me.y + dy, Y)
            block = w[:, pl.ds(pl.multiple_of(y * CHUNK, CHUNK), CHUNK)]
            part = dot(block, st[...].reshape(texts, student), 0, 0)
            ip[pl.ds(y * X, X)] = part.astype(BF16).reshape(X, ROWS, student)
            for dx in (2, 1, 3, 0):
                if dx or dy:
                    slot = y * X + lax.rem(me.x + dx, X)
                    send(ip.at[slot], ri.at[dy * X + dx], grad_s.at[0], grad_r.at[0], me.in_plane(slot))

        give_plane(2)
        give_line(0)
        give_plane(1)
        give_line(1)
        give_plane(3)
        give_plane(0)

        for g, (where, mine, _, (msg, got)) in enumerate(groups):
            share = jnp.exp2(got[:, 0:4, :] - lse_t[g][None])
            loss = jnp.sum(got[:, 4:8, :] * share, axis=0) - lse_t[g] + lse_s[g]
            picked = lax.broadcasted_iota(jnp.int32, loss.shape, 0) == lax.div(mine, 4)
            row = jnp.sum(jnp.where(picked, loss, 0.0), axis=0, keepdims=True)
            turned = pltpu.roll(jnp.broadcast_to(row, (8, 128)), lax.rem(128 - lax.rem(mine, 4) * ROWS, 128), 1)
            (row_out, col_out)[g][...] = turned

        ri[0] = ip[mine_p]
        rt[0] = tc[me.z]
        wait_for(ri.at[pl.ds(1, PLANE - 1)], grad_r.at[0])
        image_out[...] = jnp.sum(ri[...].astype(F32), axis=0)
        wait_for(rt.at[pl.ds(1, Z - 1)], grad_r.at[1])
        text_out[...] = jnp.sum(rt[...].astype(F32), axis=0)
        for n in range(2):
            wait_for(tsib.at[pl.ds(0, cut)], sib_s.at[n])
        wait_for(ri.at[pl.ds(1, PLANE - 1)], grad_s.at[0])
        wait_for(rt.at[pl.ds(1, Z - 1)], grad_s.at[1])

    if stage >= 3:
        for g, (where, mine, *pair) in enumerate(groups):
            for n in range(2):
                wait_for(pair[n][1].at[pl.ds(1, 15)], small_s.at[n, g])
    student_in.end()
    teacher_in.end()


def body(teacher_image, teacher_text, student_image, student_text, stage=4):
    teacher, student = teacher_text.shape[1], student_text.shape[1]
    texts, images = LINE * ROWS, PLANE * ROWS
    chunks = texts // CHUNK
    vmem = pltpu.VMEM
    dma = pltpu.SemaphoreType.DMA
    tile = vmem((texts, images), F32)
    grads = vmem((Z, ROWS, student), BF16)
    args = (teacher_image, teacher_text, student_image, student_text)
    image_sum, text_sum, row, col = pl.pallas_call(
        functools.partial(kernel, stage),
        out_shape=(
            jax.ShapeDtypeStruct((ROWS, student), F32),
            jax.ShapeDtypeStruct((ROWS, student), F32),
            jax.ShapeDtypeStruct((8, 128), F32),
            jax.ShapeDtypeStruct((8, 128), F32),
        ),
        in_specs=[pl.BlockSpec(memory_space=pltpu.HBM)] * 4,
        out_specs=(pl.BlockSpec(memory_space=pltpu.VMEM),) * 4,
        scratch_shapes=[
            vmem((LINE, ROWS, teacher), BF16),
            vmem((LINE, ROWS, student), BF16),
            vmem((PLANE,) + teacher_image.shape, BF16),
            vmem((PLANE,) + student_image.shape, BF16),
            tile,
            tile,
            tile,
            tile,
            tile,
            vmem((texts, images), BF16),
            vmem((2, texts, 1), F32),
            vmem((2, chunks, images), F32),
            vmem((2, chunks, images), F32),
            vmem((chunks, images), F32),
            vmem((4, 128), F32),
            vmem((4, 128), F32),
            vmem((8, 128), F32),
            vmem((8, 128), F32),
            vmem((16, 4, 128), F32),
            vmem((16, 4, 128), F32),
            vmem((16, 8, 128), F32),
            vmem((16, 8, 128), F32),
            vmem((4, 128), F32),
            vmem((Z, ROWS, student), F32),
            grads,
            grads,
            grads,
            vmem((PLANE, ROWS, student), BF16),
            grads,
            vmem((PLANE, ROWS, student), BF16),
            dma((4,)),
            dma((2, 2)),
            dma((2, 7)),
            dma((2, 7)),
            dma((2,)),
            dma((2, 2)),
            dma((2, 2)),
            dma((2,)),
            dma((2,)),
            dma((2,)),
            dma((2,)),
        ],
        compiler_params=pltpu.CompilerParams(
            collective_id=0, has_side_effects=True, vmem_limit_bytes=40 * 1024 * 1024
        ),
        name="distill",
    )(*[pltpu.with_memory_space_constraint(a, pltpu.HBM) for a in args])
    scale = 1.0 / math.sqrt(student)
    log2 = math.log(2.0)
    return (image_sum * scale, text_sum * scale, row[0, :ROWS] * log2, col[0, :ROWS] * log2)


def solution(mesh):
    in_specs = (P("grp", "blk"), P(("blk", "grp"), None), P("grp", "blk"), P(("blk", "grp"), None))
    out_specs = (
        P(("blk", "grp"), None),
        P(("blk", "grp"), None),
        P(("blk", "grp")),
        P(("blk", "grp")),
    )
    return jax.shard_map(body, mesh=mesh, in_specs=in_specs, out_specs=out_specs, check_vma=False)
```

time: 762 us -> 45.5 us (0.06)
  waiting for transfers between devices: 442 us -> 0 us
  blocking collectives: 169 us -> 0 us
  matrix products: 50.8 us -> 0 us
  starting transfers between devices: 44.2 us -> 0 us
  Pallas kernels: 0 us -> 43.6 us
  other arithmetic: 18.4 us -> 1.18 us
  between operations: 15 us -> 0.64 us
  local copies, waits for them, and re-layouts: 12.8 us -> 0 us
    ppermute x192 -> x0, waiting for transfers between devices: 425 us -> none  [shifted(): lax.ppermute(array, axis, [(i, (i + by) % length) for i in range(length)])]
    all_gather x7 -> x0, blocking collectives: 154 us -> none  [the longest x1 56.9 us: body(): every_lse = lax.all_gather(own_lse, 'blk', axis=1, tiled=True)]
    dot_general x192 -> x0, matrix products: 50.8 us -> none  [the longest x128 36.1 us: similarity(): lax.dot_general(left, right, (((1,), (0,)), ((), ())), preferred_element_...]
    pallas_call x0 -> x1, Pallas kernels: none -> 43.6 us  [body(): pl.pallas_call(functools.partial(kernel, stage), out_shape=(jax.ShapeDtyp...]
    ppermute x192 -> x0, starting transfers between devices: 33.7 us -> none  [shifted(): lax.ppermute(array, axis, [(i, (i + by) % length) for i in range(length)])]
    reduce_scatter x1 -> x0, waiting for transfers between devices: 17.3 us -> none  [body(): lax.psum_scatter(image_acc, 'grp', scatter_dimension=0, tiled=True)]
    unnamed x1 -> x0, blocking collectives: 14.6 us -> none
    reduce_sum x66 -> x0, other arithmetic: 12.2 us -> none  [the longest x64 12.1 us: tile_stats(): jnp.sum(jnp.exp(logits - jnp.expand_dims(highest, axis)), axis=axis)]
  transfers between devices with their start and end apart: 194 -> 0, of which waited for: 65 -> 0; matrix products, arithmetic and copies ran while one was open for 9% -> 0% of each run, Pallas kernels for 0% -> 0%
where the time goes in v2:
time: 45.5 us; the launch traced here: 45.4 us
  Pallas kernels  43.6 us (96%)
  other arithmetic  1.18 us (3%)
  between operations  0.64 us (1%)
    pallas_call x1, Pallas kernels, body(): pl.pallas_call(functools.partial(kernel, stage), out_shape=(jax.ShapeDtyp...  43.6 us

profile of v2, /device:TPU:1, one launch (start us, length us, event | category | flops | bytes accessed | tf_op | source)
XLA Modules:
  0.0 45.4 jit_solution(3906603832128043539)
XLA Ops:
  0.6 43.6 %distill.1 = (f32[32,512]{1,0:T(8,128)S(1)}, f32[32,512]{1,0:T(8,128)S(1)}, f32[8,128]{1,0:T(8,128)S(1)}, f32[8,128]{1,0:T(8,128)S(1)}) custom-call(bf16[160,256]{1,0:T(8,128)(2,1)} %ti_hbm.1, bf16[32,1280]{1,0:T(8,128)(2,1)} %tt_hbm.1, bf16[64,256]{1,0:T(8,128)(2,1)} %si_hbm.1, bf16[32,512]{1,0:T(8,128)(2,1)} %st_hbm.1), custom_call_target="tpu_custom_call" | custom-call | tf_op jit(solution)/shard_map/distill/pallas_call | solution.py:429
  44.2 0.5 %multiply_bitcast_fusion = (f32[32]{0:T(128)}, f32[32]{0:T(128)}) fusion(f32[8,128]{1,0:T(8,128)S(1)} %get-tuple-element.11, f32[8,128]{1,0:T(8,128)S(1)} %get-tuple-element.10), kind=kLoop, calls=%fused_computation.2 | loop fusion | flops 64 | bytes 512 | tf_op jit(solution)/shard_map/mul | solution.py:489
  44.7 0.7 %broadcast_multiply_fusion = (f32[32,512]{1,0:T(8,128)}, f32[32,512]{1,0:T(8,128)}) fusion(f32[32,512]{1,0:T(8,128)S(1)} %get-tuple-element.9, f32[32,512]{1,0:T(8,128)S(1)} %get-tuple-element.8), kind=kLoop, calls=%fused_computation | loop fusion | flops 32768 | bytes 262144 | tf_op jit(solution)/shard_map/mul | solution.py:489

commit v3 on v2

--- a/solution.py
+++ b/solution.py
@@ -38,6 +38,10 @@
 
     def in_line(self, slot):
         return self.at(z=slot % Z, core=slot // Z)
+
+
+def far(by, size):
+    return min(by, size - by)
 
 
 def wait_for(ref, sem):
@@ -58,8 +62,9 @@
 class Gather:
     NEAR = (2, -1, 1)
 
-    def __init__(self, me, texts, images, send_sem, line_r, plane_r, other_r):
+    def __init__(self, me, own_texts, own_images, texts, images, send_sem, line_r, plane_r, other_r):
         self.me, self.texts, self.images = me, texts, images
+        self.own_texts, self.own_images = own_texts, own_images
         self.ss, self.line_r, self.plane_r, self.other = send_sem, line_r, plane_r, other_r
 
     def text(self, dz):
@@ -70,46 +75,54 @@
         me = self.me
         return self.images.at[lax.rem(me.y + dy + Y, Y) * X + lax.rem(me.x + dx + X, X)]
 
-    def up(self, ref, sem, by):
+    def up(self, ref, sem, by, src=None):
         me = self.me
-        send(ref, ref, self.ss.at[0], self.line_r.at[sem], me.at(z=lax.rem(me.z + by + Z, Z)))
-
-    def share(self, dz):
+        send(ref if src is None else src, ref, self.ss.at[0], self.line_r.at[sem], me.at(z=lax.rem(me.z + by + Z, Z)))
+
+    def share(self, dz, src=None):
         ref = self.text(dz)
-        send(ref, ref, self.ss.at[0], self.other, self.me.at(core=1 - self.me.core))
-
-    def over(self, ref, sem, axis, by):
+        send(ref if src is None else src, ref, self.ss.at[0], self.other, self.me.at(core=1 - self.me.core))
+
+    def over(self, ref, sem, axis, by, src=None):
         me = self.me
         if axis == 0:
             to = me.at(x=lax.rem(me.x + by + X, X))
         else:
             to = me.at(y=lax.rem(me.y + by + Y, Y))
-        send(ref, ref, self.ss.at[1], self.plane_r.at[sem], to)
+        send(ref if src is None else src, ref, self.ss.at[1], self.plane_r.at[sem], to)
+
+    def part(self, block, axis):
+        rows = self.images.shape[1] // 2
+        return block.at[pl.ds(axis * rows, rows)]
 
     def plane_begin(self):
         own = self.image(0, 0)
         for n, by in enumerate((2, 1, -1)):
-            self.over(own, n, 0, by)
-            self.over(own, 3 + n, 1, by)
+            for axis in range(2):
+                self.over(self.part(own, axis), 3 * axis + n, axis, by, self.part(self.own_images, axis))
+
+    def plane_rest(self):
+        own = self.image(0, 0)
+        for by in (2, 1, -1):
+            for axis in range(2):
+                self.over(self.part(own, 1 - axis), 6, axis, by, self.part(self.own_images, 1 - axis))
 
     def line_far(self):
         own = self.text(0)
-        self.up(own, 0, 2)
-        self.up(own, 1, -2)
+        self.up(own, 0, 2, self.own_texts)
+        self.up(own, 1, -2, self.own_texts)
 
     def line_near(self):
         own = self.text(0)
-        self.up(own, 2, 1)
-        self.up(own, 3, -1)
-        self.share(0)
+        self.up(own, 2, 1, self.own_texts)
+        self.up(own, 3, -1, self.own_texts)
+        self.share(0, self.own_texts)
 
     def plane_turn(self):
-        rows = self.images.shape[1] // 2
         for n, by in enumerate(self.NEAR):
             for axis in range(2):
-                block = self.image(by, 0) if axis == 0 else self.image(0, by)
-                wait_for(block, self.plane_r.at[3 * axis + n])
-                part = block.at[pl.ds(axis * rows, rows)]
+                part = self.part(self.image(by, 0) if axis == 0 else self.image(0, by), axis)
+                wait_for(part, self.plane_r.at[3 * axis + n])
                 for to in (2, 1, -1):
                     self.over(part, 6, 1 - axis, to)
 
@@ -124,6 +137,8 @@
         self.up(b, 5, -1)
         self.share(-2)
         self.share(2)
+
+    def line_share(self):
         wait_for(self.text(-1), self.line_r.at[2])
         wait_for(self.text(1), self.line_r.at[3])
         self.share(-1)
@@ -137,8 +152,10 @@
         wait_for(self.text(4), self.line_r.at[6])
         self.share(4)
 
-    def finish(self):
-        wait_for(self.images.at[pl.ds(0, 9)], self.plane_r.at[6])
+    def plane_finish(self):
+        wait_for(self.images.at[pl.ds(0, 12)], self.plane_r.at[6])
+
+    def other_finish(self):
         wait_for(self.texts.at[pl.ds((1 - self.me.core) * Z, Z)], self.other)
 
     def end(self):
@@ -172,9 +189,10 @@
     stage,
     ti_hbm, tt_hbm, si_hbm, st_hbm,
     image_out, text_out, row_out, col_out,
-    tt, st, it, is_, s2, ert, ect, ers, ecs, w, col_max, row_max, row_sum, row_kl,
-    s_line, s_plane, t_line, t_plane, gs_line, gs_plane, gt_line, gt_plane, col_lse,
-    tp, tsend, tsib, tc, ip, rt, ri,
+    tt, st, it, is_, s2, t2, ert, ect, ers, ecs, w, col_max, col_sum, row_max, row_sum,
+    s_line, s_plane, t_line, t_plane, k_line, k_plane,
+    gs_line, gs_plane, gt_line, gt_plane, gk_line, gk_plane, col_lse,
+    tp, tsend, tsib, tc, ip, ip0, rt, ri,
     local_sem, gather_sem, line_r, plane_r, other_r,
     small_s, small_r, sib_s, sib_r, grad_s, grad_r,
 ):
@@ -193,8 +211,6 @@
         pltpu.make_async_copy(st_hbm, st.at[mine_l], local_sem.at[2]),
         pltpu.make_async_copy(si_hbm, is_.at[mine_p], local_sem.at[3]),
     ]
-    for copy in own:
-        copy.start()
     barrier = pltpu.get_barrier_semaphore()
 
     near = [me.at(core=1 - me.core)]
@@ -204,20 +220,25 @@
     for device in near:
         pl.semaphore_signal(barrier, inc=1, device_id=device, device_id_type=MESH)
     for copy in own:
-        copy.wait()
+        copy.start()
     pl.semaphore_wait(barrier, len(near))
 
-    teacher_in = Gather(me, tt, it, gather_sem.at[0], line_r.at[0], plane_r.at[0], other_r.at[0])
-    student_in = Gather(me, st, is_, gather_sem.at[1], line_r.at[1], plane_r.at[1], other_r.at[1])
+    teacher_in = Gather(me, tt_hbm, ti_hbm, tt, it, gather_sem.at[0], line_r.at[0], plane_r.at[0], other_r.at[0])
+    student_in = Gather(me, st_hbm, si_hbm, st, is_, gather_sem.at[1], line_r.at[1], plane_r.at[1], other_r.at[1])
     both = (student_in, teacher_in)
     for g in both:
         g.line_far()
         g.plane_begin()
     for g in both:
+        g.plane_rest()
         g.line_near()
     for g in both:
         g.plane_turn()
         g.line_turn()
+    for g in both:
+        g.line_share()
+    for copy in own:
+        copy.wait()
 
     def tiles_of(k, texts_buf, image_buf):
         width = texts_buf.shape[2]
@@ -255,31 +276,41 @@
         for a in range(4):
             ref[first + a : first + a + 1, :] = lanes[:, a * 128 : a * 128 + 128]
 
-    groups = (me.in_plane, mine_p, (s_plane, gs_plane), (t_plane, gt_plane)), (
-        me.in_line, mine_l, (s_line, gs_line), (t_line, gt_line))
+    planes = sorted(((dx, dy) for dx in range(X) for dy in range(Y) if dx or dy), key=lambda o: -far(o[0], X) - far(o[1], Y))
+    lines = sorted(((dz, dc) for dz in range(Z) for dc in range(2) if dz or dc), key=lambda o: -far(o[0], Z))
+    groups = ((s_plane, gs_plane), (t_plane, gt_plane), (k_plane, gk_plane)), (
+        (s_line, gs_line), (t_line, gt_line), (k_line, gk_line))
 
     def tell(n):
-        def one(d, carry):
-            for g, (where, mine, *pair) in enumerate(groups):
-                msg, got = pair[n]
-                send(msg, got.at[d], small_s.at[n, g], small_r.at[n, g], where((mine + d) % 16))
-            return carry
-
-        lax.fori_loop(1, 16, one, 0)
+        for (dx, dy), (dz, dc) in zip(planes, lines):
+            msg, got = groups[0][n]
+            to = me.at(x=lax.rem(me.x + dx, X), y=lax.rem(me.y + dy, Y))
+            send(msg, got.at[dy * X + dx], small_s.at[n, 0], small_r.at[n, 0], to)
+            msg, got = groups[1][n]
+            to = me.at(z=lax.rem(me.z + dz, Z), core=lax.rem(me.core + dc, 2))
+            send(msg, got.at[dc * Z + dz], small_s.at[n, 1], small_r.at[n, 1], to)
 
     def hear(n, g):
-        msg, got = groups[g][2 + n]
+        msg, got = groups[g][n]
         got[0] = msg[...]
         wait_for(got.at[pl.ds(1, 15)], small_r.at[n, g])
-        every = got[:, 0:4, :]
+        every = got[...]
         top = jnp.max(every, axis=0)
         return top + jnp.log2(jnp.sum(jnp.exp2(every - top[None]), axis=0))
 
+    def by_core(source, step):
+        per_core = chunks // 2
+        for core in (me.core, 1 - me.core):
+            for k in range(per_core):
+                step(core * per_core + k)
+            if core is me.core:
+                source.other_finish()
+
     student_in.line_finish()
-    student_in.finish()
+    student_in.plane_finish()
     if stage >= 2:
 
-        def student_chunk(k, carry):
+        def student_chunk(k):
             tiles = tiles_of(k, st, is_)
 
             def seen(rows, cols, tile, e_row, e_col):
@@ -287,37 +318,39 @@
 
             lse, _ = stats(k, 1, tiles, ers, ecs, seen)
             s_line[pl.ds(k, 1), :] = to_lanes(lse)
-            return carry
-
-        lax.fori_loop(0, chunks, student_chunk, 0)
+
+        by_core(student_in, student_chunk)
         lay(s_plane, 0, row_stats(1)[0])
     if stage >= 3:
         tell(0)
     teacher_in.line_finish()
-    teacher_in.finish()
+    teacher_in.plane_finish()
     if stage >= 2:
 
-        def teacher_chunk(k, carry):
+        def teacher_chunk(k):
             tiles = tiles_of(k, tt, it)
-            kls = []
 
             def seen(rows, cols, tile, e_row, e_col):
-                gap = tile - s2[rows, cols]
-                kls.append(e_col * gap)
-                row_kl[pl.ds(k, 1), cols] = jnp.sum(e_row * gap, axis=0, keepdims=True)
+                t2[rows, cols] = tile
 
             lse, total = stats(k, 0, tiles, ert, ect, seen)
+            col_sum[pl.ds(pl.multiple_of(k * CHUNK, CHUNK), CHUNK)] = total
             t_line[pl.ds(k, 1), :] = to_lanes(lse)
-            kl = jnp.sum(functools.reduce(jnp.add, kls), axis=1, keepdims=True)
-            t_line[pl.ds(4 + k, 1), :] = to_lanes(kl / total)
-            return carry
-
-        lax.fori_loop(0, chunks, teacher_chunk, 0)
+
+        by_core(teacher_in, teacher_chunk)
         lse, part, total = row_stats(0)
         lay(t_plane, 0, lse)
-        lay(t_plane, 4, jnp.sum(row_kl[...] * part, axis=0, keepdims=True) / total)
     if stage >= 3:
         tell(1)
+        row_kl = jnp.zeros((1, images), F32)
+        for k in range(chunks):
+            rows = pl.ds(k * CHUNK, CHUNK)
+            gap = t2[rows, :] - s2[rows, :]
+            row_kl += jnp.sum(ert[rows, :] * gap, axis=0, keepdims=True) * part[k : k + 1, :]
+            kl = jnp.sum(ect[rows, :] * gap, axis=1, keepdims=True) / col_sum[rows]
+            k_line[pl.ds(k, 1), :] = to_lanes(kl)
+        lay(k_plane, 0, row_kl / total)
+        tell(2)
         lse_s = [hear(0, 0), hear(0, 1)]
         if stage >= 4:
             image_lse = across([lse_s[0][a : a + 1, :] for a in range(4)])
@@ -342,36 +375,28 @@
             rows = pl.ds(pl.multiple_of(k * CHUNK, CHUNK), CHUNK)
             by_row = jnp.exp2(row_max[0, pl.ds(k, 1), :] - image_lse) * pairs
             by_col = jnp.exp2(col_max[0, rows] - to_rows(col_lse[pl.ds(k, 1), :])) * pairs
-            weights = (ers[rows, :] - ert[rows, :] * by_row - ect[rows, :] * by_col).astype(BF16)
-            w[rows, :] = weights
+            w[rows, :] = (ers[rows, :] - ert[rows, :] * by_row - ect[rows, :] * by_col).astype(BF16)
+
+        def text_part(k):
+            rows = pl.ds(pl.multiple_of(k * CHUNK, CHUNK), CHUNK)
             parts = [
-                dot(weights[:, a * 256 : a * 256 + 256], is_[pl.ds(a * 8, 8)].reshape(student, 256), 1, 1)
+                dot(w[rows, pl.ds(a * 256, 256)], is_[pl.ds(a * 8, 8)].reshape(student, 256), 1, 1)
                 for a in range(images // 256)
             ]
             return functools.reduce(jnp.add, parts).reshape(cut, ROWS, student)
 
-        half = lax.div(me.z, 4)
-
-        def part_of(n):
-            h = lax.rem(half + 1 + n, 2)
-            return h, pl.ds(h * cut, cut)
-
-        for n in range(2):
-            h, part = part_of(n)
-            tsend[part] = weigh(other * 2 + h).astype(BF16)
-            send(tsend.at[part], tsib.at[part], sib_s.at[n], sib_r.at[n], me.at(core=other))
-        for n in range(2):
-            h, part = part_of(n)
-            tp[part] = weigh(me.core * 2 + h)
+        per_core = chunks // 2
 
         def give_line(n):
-            h, part = part_of(n)
+            part = pl.ds(n * cut, cut)
             wait_for(tsib.at[part], sib_r.at[n])
             tc[part] = (tp[part] + tsib[part].astype(F32)).astype(BF16)
-            for i in range(n, 4):
-                z = h * 4 + lax.rem(me.z + i, 4)
-                d = lax.rem(z - me.z + Z, Z)
-                send(tc.at[z], rt.at[d], grad_s.at[1], grad_r.at[1], me.at(z=z))
+            for z in range(n * cut, (n + 1) * cut):
+
+                @pl.when(me.z != z)
+                def _():
+                    to = rt.at[lax.rem(z - me.z + Z, Z)]
+                    send(tc.at[z], to, grad_s.at[1], grad_r.at[1], me.at(z=z))
 
         def give_plane(dy):
             y = lax.rem(me.y + dy, Y)
@@ -381,18 +406,47 @@
             for dx in (2, 1, 3, 0):
                 if dx or dy:
                     slot = y * X + lax.rem(me.x + dx, X)
-                    send(ip.at[slot], ri.at[dy * X + dx], grad_s.at[0], grad_r.at[0], me.in_plane(slot))
+
+                    @pl.when(jnp.logical_or(slot != 0, me.z != 0))
+                    def _():
+                        send(ip.at[slot], ri.at[dy * X + dx], grad_s.at[0], grad_r.at[0], me.in_plane(slot))
+
+        def swap(n):
+            part = pl.ds(n * cut, cut)
+            tsend[part] = text_part(other * per_core + n).astype(BF16)
+            send(tsend.at[part], tsib.at[part], sib_s.at[n], sib_r.at[n], me.at(core=other))
+
+        def keep(n):
+            tp[pl.ds(n * cut, cut)] = text_part(me.core * per_core + n)
+
+        weigh(other * per_core)
+        swap(0)
+        weigh(me.core * per_core)
+        weigh(other * per_core + 1)
+        weigh(me.core * per_core + 1)
+        @pl.when(jnp.logical_and(me.z == 0, mine_p != 0))
+        def _():
+            part = dot(w[:, :CHUNK], st[...].reshape(texts, student), 0, 0)
+            ip0[...] = part[:ROWS].astype(BF16)
+            to = ri.at[lax.rem(Y - me.y, Y) * X + lax.rem(X - me.x, X)]
+            send(ip0, to, grad_s.at[0], grad_r.at[0], me.in_plane(0))
 
         give_plane(2)
+        swap(1)
+        keep(0)
+        give_plane(1)
         give_line(0)
-        give_plane(1)
+        give_plane(3)
+        keep(1)
+        give_plane(0)
         give_line(1)
-        give_plane(3)
-        give_plane(0)
-
-        for g, (where, mine, _, (msg, got)) in enumerate(groups):
-            share = jnp.exp2(got[:, 0:4, :] - lse_t[g][None])
-            loss = jnp.sum(got[:, 4:8, :] * share, axis=0) - lse_t[g] + lse_s[g]
+
+        for g, (_, (_, got_t), (msg, got)) in enumerate(groups):
+            mine = (mine_p, mine_l)[g]
+            got[0] = msg[...]
+            wait_for(got.at[pl.ds(1, 15)], small_r.at[2, g])
+            share = jnp.exp2(got_t[...] - lse_t[g][None])
+            loss = jnp.sum(got[...] * share, axis=0) - lse_t[g] + lse_s[g]
             picked = lax.broadcasted_iota(jnp.int32, loss.shape, 0) == lax.div(mine, 4)
             row = jnp.sum(jnp.where(picked, loss, 0.0), axis=0, keepdims=True)
             turned = pltpu.roll(jnp.broadcast_to(row, (8, 128)), lax.rem(128 - lax.rem(mine, 4) * ROWS, 128), 1)
@@ -409,10 +463,15 @@
         wait_for(ri.at[pl.ds(1, PLANE - 1)], grad_s.at[0])
         wait_for(rt.at[pl.ds(1, Z - 1)], grad_s.at[1])
 
+    if stage == 1:
+        student_in.other_finish()
+        teacher_in.other_finish()
     if stage >= 3:
-        for g, (where, mine, *pair) in enumerate(groups):
-            for n in range(2):
-                wait_for(pair[n][1].at[pl.ds(1, 15)], small_s.at[n, g])
+        for g in range(2):
+            for n in range(3):
+                wait_for(groups[g][n][1].at[pl.ds(1, 15)], small_s.at[n, g])
+            if stage == 3:
+                wait_for(groups[g][2][1].at[pl.ds(1, 15)], small_r.at[2, g])
     student_in.end()
     teacher_in.end()
 
@@ -446,25 +505,21 @@
             tile,
             tile,
             tile,
+            tile,
             vmem((texts, images), BF16),
             vmem((2, texts, 1), F32),
+            vmem((texts, 1), F32),
             vmem((2, chunks, images), F32),
             vmem((2, chunks, images), F32),
-            vmem((chunks, images), F32),
-            vmem((4, 128), F32),
-            vmem((4, 128), F32),
-            vmem((8, 128), F32),
-            vmem((8, 128), F32),
-            vmem((16, 4, 128), F32),
-            vmem((16, 4, 128), F32),
-            vmem((16, 8, 128), F32),
-            vmem((16, 8, 128), F32),
+            *[vmem((4, 128), F32)] * 6,
+            *[vmem((16, 4, 128), F32)] * 6,
             vmem((4, 128), F32),
             vmem((Z, ROWS, student), F32),
             grads,
             grads,
             grads,
             vmem((PLANE, ROWS, student), BF16),
+            vmem((ROWS, student), BF16),
             grads,
             vmem((PLANE, ROWS, student), BF16),
             dma((4,)),
@@ -472,8 +527,8 @@
             dma((2, 7)),
             dma((2, 7)),
             dma((2,)),
-            dma((2, 2)),
-            dma((2, 2)),
+            dma((3, 2)),
+            dma((3, 2)),
             dma((2,)),
             dma((2,)),
             dma((2,)),

time: 45.5 us -> 41.8 us (0.919)
  Pallas kernels: 43.6 us -> 39.9 us
    pallas_call x1, Pallas kernels: 43.6 us -> 39.9 us  [body(): pl.pallas_call(functools.partial(kernel, stage), out_shape=(jax.ShapeDtyp...]
where the time goes in v3:
time: 41.8 us; the launch traced here: 41.7 us
  Pallas kernels  39.9 us (95%)
  other arithmetic  1.18 us (3%)
  between operations  0.64 us (2%)
    pallas_call x1, Pallas kernels, body(): pl.pallas_call(functools.partial(kernel, stage), out_shape=(jax.ShapeDtyp...  39.9 us

profile of v3, /device:TPU:1, one launch (start us, length us, event | category | flops | bytes accessed | tf_op | source)
XLA Modules:
  0.0 41.7 jit_solution(2764463963069216245)
XLA Ops:
  0.6 39.9 %distill.1 = (f32[32,512]{1,0:T(8,128)S(1)}, f32[32,512]{1,0:T(8,128)S(1)}, f32[8,128]{1,0:T(8,128)S(1)}, f32[8,128]{1,0:T(8,128)S(1)}) custom-call(bf16[160,256]{1,0:T(8,128)(2,1)} %ti_hbm.1, bf16[32,1280]{1,0:T(8,128)(2,1)} %tt_hbm.1, bf16[64,256]{1,0:T(8,128)(2,1)} %si_hbm.1, bf16[32,512]{1,0:T(8,128)(2,1)} %st_hbm.1), custom_call_target="tpu_custom_call" | custom-call | tf_op jit(solution)/shard_map/distill/pallas_call | solution.py:488
  40.5 0.5 %multiply_bitcast_fusion = (f32[32]{0:T(128)}, f32[32]{0:T(128)}) fusion(f32[8,128]{1,0:T(8,128)S(1)} %get-tuple-element.11, f32[8,128]{1,0:T(8,128)S(1)} %get-tuple-element.10), kind=kLoop, calls=%fused_computation.2 | loop fusion | flops 64 | bytes 512 | tf_op jit(solution)/shard_map/mul | solution.py:544
  41.1 0.7 %broadcast_multiply_fusion = (f32[32,512]{1,0:T(8,128)}, f32[32,512]{1,0:T(8,128)}) fusion(f32[32,512]{1,0:T(8,128)S(1)} %get-tuple-element.9, f32[32,512]{1,0:T(8,128)S(1)} %get-tuple-element.8), kind=kLoop, calls=%fused_computation | loop fusion | flops 32768 | bytes 262144 | tf_op jit(solution)/shard_map/mul | solution.py:544

commit v4 on v3

--- a/solution.py
+++ b/solution.py
@@ -107,10 +107,17 @@
             for axis in range(2):
                 self.over(self.part(own, 1 - axis), 6, axis, by, self.part(self.own_images, 1 - axis))
 
+    def halves(self, block):
+        half = ROWS // 2
+        return block.at[pl.ds(0, half)], block.at[pl.ds(half, half)]
+
     def line_far(self):
-        own = self.text(0)
-        self.up(own, 0, 2, self.own_texts)
-        self.up(own, 1, -2, self.own_texts)
+        first, second = self.halves(self.text(0))
+        own_first, own_second = self.halves(self.own_texts)
+        self.up(first, 0, 2, own_first)
+        self.up(second, 1, -2, own_second)
+        self.up(second, 7, 2, own_second)
+        self.up(first, 8, -2, own_first)
 
     def line_near(self):
         own = self.text(0)
@@ -126,13 +133,28 @@
                 for to in (2, 1, -1):
                     self.over(part, 6, 1 - axis, to)
 
-    def line_turn(self):
-        half = ROWS // 2
+    def line_next(self):
+        a, b = self.text(-1), self.text(1)
+        wait_for(a, self.line_r.at[2])
+        wait_for(b, self.line_r.at[3])
+        self.up(a, 0, 1)
+        self.up(b, 1, -1)
+        self.share(-1)
+        self.share(1)
+
+    def line_turn(self, halves):
         a, b = self.text(-2), self.text(2)
-        wait_for(a, self.line_r.at[0])
-        wait_for(b, self.line_r.at[1])
-        self.up(a.at[pl.ds(0, half)], 6, 2)
-        self.up(b.at[pl.ds(half, half)], 6, -2)
+        first, second = self.halves(a)[0], self.halves(b)[1]
+        wait_for(first if halves else a, self.line_r.at[0])
+        self.up(first, 6, 2)
+        wait_for(second if halves else b, self.line_r.at[1])
+        self.up(second, 6, -2)
+
+    def line_last(self, halves):
+        a, b = self.text(-2), self.text(2)
+        if halves:
+            wait_for(self.halves(a)[1], self.line_r.at[7])
+            wait_for(self.halves(b)[0], self.line_r.at[8])
         self.up(a, 4, 1)
         self.up(b, 5, -1)
         self.share(-2)
@@ -225,18 +247,21 @@
 
     teacher_in = Gather(me, tt_hbm, ti_hbm, tt, it, gather_sem.at[0], line_r.at[0], plane_r.at[0], other_r.at[0])
     student_in = Gather(me, st_hbm, si_hbm, st, is_, gather_sem.at[1], line_r.at[1], plane_r.at[1], other_r.at[1])
-    both = (student_in, teacher_in)
-    for g in both:
-        g.line_far()
-        g.plane_begin()
-    for g in both:
-        g.plane_rest()
-        g.line_near()
-    for g in both:
-        g.plane_turn()
-        g.line_turn()
-    for g in both:
-        g.line_share()
+    student_in.line_near()
+    teacher_in.line_far()
+    student_in.plane_begin()
+    teacher_in.plane_begin()
+    student_in.plane_rest()
+    teacher_in.plane_rest()
+    student_in.line_next()
+    teacher_in.line_near()
+    student_in.plane_turn()
+    teacher_in.plane_turn()
+    student_in.line_turn(False)
+    student_in.line_last(False)
+    teacher_in.line_turn(True)
+    teacher_in.line_last(True)
+    teacher_in.line_share()
     for copy in own:
         copy.wait()
 
@@ -281,12 +306,15 @@
     groups = ((s_plane, gs_plane), (t_plane, gt_plane), (k_plane, gk_plane)), (
         (s_line, gs_line), (t_line, gt_line), (k_line, gk_line))
 
-    def tell(n):
-        for (dx, dy), (dz, dc) in zip(planes, lines):
-            msg, got = groups[0][n]
+    def tell_plane(n):
+        msg, got = groups[0][n]
+        for dx, dy in planes:
             to = me.at(x=lax.rem(me.x + dx, X), y=lax.rem(me.y + dy, Y))
             send(msg, got.at[dy * X + dx], small_s.at[n, 0], small_r.at[n, 0], to)
-            msg, got = groups[1][n]
+
+    def tell_line(n):
+        msg, got = groups[1][n]
+        for dz, dc in lines:
             to = me.at(z=lax.rem(me.z + dz, Z), core=lax.rem(me.core + dc, 2))
             send(msg, got.at[dc * Z + dz], small_s.at[n, 1], small_r.at[n, 1], to)
 
@@ -320,9 +348,11 @@
             s_line[pl.ds(k, 1), :] = to_lanes(lse)
 
         by_core(student_in, student_chunk)
+        if stage >= 3:
+            tell_line(0)
         lay(s_plane, 0, row_stats(1)[0])
-    if stage >= 3:
-        tell(0)
+        if stage >= 3:
+            tell_plane(0)
     teacher_in.line_finish()
     teacher_in.plane_finish()
     if stage >= 2:
@@ -338,10 +368,12 @@
             t_line[pl.ds(k, 1), :] = to_lanes(lse)
 
         by_core(teacher_in, teacher_chunk)
+        if stage >= 3:
+            tell_line(1)
         lse, part, total = row_stats(0)
         lay(t_plane, 0, lse)
     if stage >= 3:
-        tell(1)
+        tell_plane(1)
         row_kl = jnp.zeros((1, images), F32)
         for k in range(chunks):
             rows = pl.ds(k * CHUNK, CHUNK)
@@ -350,7 +382,8 @@
             kl = jnp.sum(ect[rows, :] * gap, axis=1, keepdims=True) / col_sum[rows]
             k_line[pl.ds(k, 1), :] = to_lanes(kl)
         lay(k_plane, 0, row_kl / total)
-        tell(2)
+        tell_plane(2)
+        tell_line(2)
         lse_s = [hear(0, 0), hear(0, 1)]
         if stage >= 4:
             image_lse = across([lse_s[0][a : a + 1, :] for a in range(4)])
@@ -524,7 +557,7 @@
             vmem((PLANE, ROWS, student), BF16),
             dma((4,)),
             dma((2, 2)),
-            dma((2, 7)),
+            dma((2, 9)),
             dma((2, 7)),
             dma((2,)),
             dma((3, 2)),

time: 41.8 us -> 41.5 us (level)
  no operation moved by 1% of the time
where the time goes in v4:
time: 41.5 us
  Pallas kernels  39.6 us (95%)
  other arithmetic  1.18 us (3%)
  between operations  0.64 us (2%)
    pallas_call x1, Pallas kernels, body(): pl.pallas_call(functools.partial(kernel, stage), out_shape=(jax.ShapeDtyp...  39.6 us

profile of v4, /device:TPU:1, one launch (start us, length us, event | category | flops | bytes accessed | tf_op | source)
XLA Modules:
  0.0 41.5 jit_solution(6553289144378283629)
XLA Ops:
  0.6 39.6 %distill.1 = (f32[32,512]{1,0:T(8,128)S(1)}, f32[32,512]{1,0:T(8,128)S(1)}, f32[8,128]{1,0:T(8,128)S(1)}, f32[8,128]{1,0:T(8,128)S(1)}) custom-call(bf16[160,256]{1,0:T(8,128)(2,1)} %ti_hbm.1, bf16[32,1280]{1,0:T(8,128)(2,1)} %tt_hbm.1, bf16[64,256]{1,0:T(8,128)(2,1)} %si_hbm.1, bf16[32,512]{1,0:T(8,128)(2,1)} %st_hbm.1), custom_call_target="tpu_custom_call" | custom-call | tf_op jit(solution)/shard_map/distill/pallas_call | solution.py:521
  40.3 0.5 %multiply_bitcast_fusion = (f32[32]{0:T(128)}, f32[32]{0:T(128)}) fusion(f32[8,128]{1,0:T(8,128)S(1)} %get-tuple-element.11, f32[8,128]{1,0:T(8,128)S(1)} %get-tuple-element.10), kind=kLoop, calls=%fused_computation.2 | loop fusion | flops 64 | bytes 512 | tf_op jit(solution)/shard_map/mul | solution.py:577
  40.8 0.7 %broadcast_multiply_fusion = (f32[32,512]{1,0:T(8,128)}, f32[32,512]{1,0:T(8,128)}) fusion(f32[32,512]{1,0:T(8,128)S(1)} %get-tuple-element.9, f32[32,512]{1,0:T(8,128)S(1)} %get-tuple-element.8), kind=kLoop, calls=%fused_computation | loop fusion | flops 32768 | bytes 262144 | tf_op jit(solution)/shard_map/mul | solution.py:577

commit v5 on v4

--- a/solution.py
+++ b/solution.py
@@ -251,8 +251,8 @@
     teacher_in.line_far()
     student_in.plane_begin()
     teacher_in.plane_begin()
+    teacher_in.plane_rest()
     student_in.plane_rest()
-    teacher_in.plane_rest()
     student_in.line_next()
     teacher_in.line_near()
     student_in.plane_turn()

time: 41.5 us -> 41.5 us (level)
  no operation moved by 1% of the time
where the time goes in v5:
time: 41.5 us
  Pallas kernels  39.6 us (95%)
  other arithmetic  1.18 us (3%)
  between operations  0.64 us (2%)
    pallas_call x1, Pallas kernels, body(): pl.pallas_call(functools.partial(kernel, stage), out_shape=(jax.ShapeDtyp...  39.6 us

profile of v5, /device:TPU:1, one launch (start us, length us, event | category | flops | bytes accessed | tf_op | source)
XLA Modules:
  0.0 41.5 jit_solution(7265642959229937741)
XLA Ops:
  0.6 39.6 %distill.1 = (f32[32,512]{1,0:T(8,128)S(1)}, f32[32,512]{1,0:T(8,128)S(1)}, f32[8,128]{1,0:T(8,128)S(1)}, f32[8,128]{1,0:T(8,128)S(1)}) custom-call(bf16[160,256]{1,0:T(8,128)(2,1)} %ti_hbm.1, bf16[32,1280]{1,0:T(8,128)(2,1)} %tt_hbm.1, bf16[64,256]{1,0:T(8,128)(2,1)} %si_hbm.1, bf16[32,512]{1,0:T(8,128)(2,1)} %st_hbm.1), custom_call_target="tpu_custom_call" | custom-call | tf_op jit(solution)/shard_map/distill/pallas_call | solution.py:521
  40.3 0.5 %multiply_bitcast_fusion = (f32[32]{0:T(128)}, f32[32]{0:T(128)}) fusion(f32[8,128]{1,0:T(8,128)S(1)} %get-tuple-element.11, f32[8,128]{1,0:T(8,128)S(1)} %get-tuple-element.10), kind=kLoop, calls=%fused_computation.2 | loop fusion | flops 64 | bytes 512 | tf_op jit(solution)/shard_map/mul | solution.py:577
  40.8 0.7 %broadcast_multiply_fusion = (f32[32,512]{1,0:T(8,128)}, f32[32,512]{1,0:T(8,128)}) fusion(f32[32,512]{1,0:T(8,128)S(1)} %get-tuple-element.9, f32[32,512]{1,0:T(8,128)S(1)} %get-tuple-element.8), kind=kLoop, calls=%fused_computation | loop fusion | flops 32768 | bytes 262144 | tf_op jit(solution)/shard_map/mul | solution.py:577

commit v6 on v4

--- a/solution.py
+++ b/solution.py
@@ -469,10 +469,10 @@
         keep(0)
         give_plane(1)
         give_line(0)
+        keep(1)
         give_plane(3)
-        keep(1)
+        give_line(1)
         give_plane(0)
-        give_line(1)
 
         for g, (_, (_, got_t), (msg, got)) in enumerate(groups):
             mine = (mine_p, mine_l)[g]

time: 41.5 us -> 41.5 us (level)
  no operation moved by 1% of the time
where the time goes in v6:
time: 41.5 us
  Pallas kernels  39.6 us (95%)
  other arithmetic  1.18 us (3%)
  between operations  0.64 us (2%)
    pallas_call x1, Pallas kernels, body(): pl.pallas_call(functools.partial(kernel, stage), out_shape=(jax.ShapeDtyp...  39.6 us

profile of v6, /device:TPU:1, one launch (start us, length us, event | category | flops | bytes accessed | tf_op | source)
XLA Modules:
  0.0 41.5 jit_solution(10753924514695273800)
XLA Ops:
  0.6 39.6 %distill.1 = (f32[32,512]{1,0:T(8,128)S(1)}, f32[32,512]{1,0:T(8,128)S(1)}, f32[8,128]{1,0:T(8,128)S(1)}, f32[8,128]{1,0:T(8,128)S(1)}) custom-call(bf16[160,256]{1,0:T(8,128)(2,1)} %ti_hbm.1, bf16[32,1280]{1,0:T(8,128)(2,1)} %tt_hbm.1, bf16[64,256]{1,0:T(8,128)(2,1)} %si_hbm.1, bf16[32,512]{1,0:T(8,128)(2,1)} %st_hbm.1), custom_call_target="tpu_custom_call" | custom-call | tf_op jit(solution)/shard_map/distill/pallas_call | solution.py:521
  40.3 0.5 %multiply_bitcast_fusion = (f32[32]{0:T(128)}, f32[32]{0:T(128)}) fusion(f32[8,128]{1,0:T(8,128)S(1)} %get-tuple-element.11, f32[8,128]{1,0:T(8,128)S(1)} %get-tuple-element.10), kind=kLoop, calls=%fused_computation.2 | loop fusion | flops 64 | bytes 512 | tf_op jit(solution)/shard_map/mul | solution.py:577
  40.8 0.7 %broadcast_multiply_fusion = (f32[32,512]{1,0:T(8,128)}, f32[32,512]{1,0:T(8,128)}) fusion(f32[32,512]{1,0:T(8,128)S(1)} %get-tuple-element.9, f32[32,512]{1,0:T(8,128)S(1)} %get-tuple-element.8), kind=kLoop, calls=%fused_computation | loop fusion | flops 32768 | bytes 262144 | tf_op jit(solution)/shard_map/mul | solution.py:577
